TPU v7x, 256 devices: a whole 4x4x8 slice. The times are simulated.
256 devices in a mesh: expert: 32 (over z, y_hi, core), hid: 8 (over y_lo, x).
Axes of the slice: x: 4, y: 4 (y_hi: 2, y_lo: 2; y = y_hi * 2 + y_lo), z: 8, core: 2. Of those that a mesh axis runs over, the one named last changes fastest.
Arguments:
- tokens: bfloat16 [4096, 7168], P('expert', 'hid'), may hold values from -6 to 6
- cotangent: bfloat16 [4096, 7168], P('expert', 'hid'), may hold values from -6 to 6
- expert_ids: int32 [4096, 8], P('expert'), may hold values from 0 to 31, all different within a row; in each aligned block of 128 rows (0 to 127, 128 to 255, ...) at most 40 rows name the same one
- gate_weights: float32 [4096, 8], P('expert'), may hold values from 0.1 to 0.6
- owner_old: int32 [32], replicated, may hold values from 0 to 31, as said below
- owner_new: int32 [32], replicated, may hold values from 0 to 31, as said below
- w_gate: bfloat16 [32, 1024, 7168], P('expert', None, 'hid'), may hold values from -0.0625 to 0.0625
- w_down: bfloat16 [32, 1024, 7168], P('expert', None, 'hid'), may hold values from -0.1875 to 0.1875
Outputs:
- layer_out: bfloat16 [4096, 7168], P('expert', 'hid')
- token_grads: bfloat16 [4096, 7168], P('expert', 'hid')
- grad_gate: bfloat16 [32, 1024, 7168], P('expert', None, 'hid')
- grad_down: bfloat16 [32, 1024, 7168], P('expert', None, 'hid')
Inputs may be any that keep to these rules, and one draw needn't show every extreme that they name: `expert_ids`: each row names 8 different experts. Within the rows of one device (aligned blocks of 128 rows) no expert is named more than 40 times, and in some block an expert is named exactly 40 times. `owner_old`: A permutation of the experts over the device indices. `owner_new`: A permutation that agrees with owner_old on all experts but exactly 8 of them.
All inputs are finite; a program needn't handle non-finite values.
Results may differ from a plain program's by a relative error of at most 0.025.
Values may be sent and summed in bfloat16 or wider, within the bound.
A program may use at most 128 MiB of HBM per device.

v0:
```python
import jax
import jax.numpy as jnp
from jax import lax
from jax.sharding import PartitionSpec as P


def into_pieces(block_mat, piece_count):
    return block_mat.reshape(piece_count, block_mat.shape[0] // piece_count, block_mat.shape[1])


def contract_width(left_mat, right_mat):
    return lax.dot_general(
        left_mat, right_mat, (((1,), (1,)), ((), ())), preferred_element_type=jnp.float32
    )


def contract_rows(left_mat, right_mat):
    return lax.dot_general(
        left_mat, right_mat, (((0,), (0,)), ((), ())), preferred_element_type=jnp.float32
    )


def activate(pre_act, back_act):
    sigmoid_pre = jax.nn.sigmoid(pre_act)
    hidden = (pre_act * sigmoid_pre).astype(jnp.bfloat16)
    slope_rows = (back_act * sigmoid_pre * (1.0 + pre_act * (1.0 - sigmoid_pre))).astype(
        jnp.bfloat16
    )
    return (hidden, slope_rows)


def gate_side(slope_rows, rows_in, gate_here):
    gate_step = contract_rows(slope_rows, rows_in).astype(jnp.bfloat16)
    back_rows = jnp.dot(slope_rows, gate_here, preferred_element_type=jnp.float32).astype(
        jnp.bfloat16
    )
    return (gate_step, back_rows)


def per_device(tokens, cotangent, expert_ids, gate_weights, owner_old, owner_new, w_gate, w_down):
    groups = lax.axis_size("expert")
    tok_rows, top_count = expert_ids.shape
    experts_all = owner_old.shape[0]
    width_here = tokens.shape[1]
    capacity = max(2, tok_rows * top_count * 5 // (4 * groups))
    labels = jnp.arange(experts_all, dtype=jnp.int32)
    onehot = (expert_ids[:, :, None] == labels).astype(jnp.int32)
    per_token = jnp.sum(onehot, axis=1, dtype=jnp.int32)
    before = jnp.cumsum(per_token, axis=0, dtype=jnp.int32) - per_token
    slot_rank = jnp.sum(onehot * before[:, None, :], axis=2, dtype=jnp.int32)
    moved_to = (owner_new[:, None] == labels[None, :]).astype(jnp.int32)
    source_of = jnp.sum(moved_to * owner_old[:, None], axis=0, dtype=jnp.int32)
    gate_here = w_gate[0]
    down_here = w_down[0]
    target = jnp.sum(onehot * owner_old, axis=2, dtype=jnp.int32)
    position = target * capacity + slot_rank
    pair_ids = jnp.arange(tok_rows * top_count, dtype=jnp.int32)
    filler = (
        jnp.full((groups * capacity,), tok_rows * top_count, jnp.int32)
        .at[position.reshape(-1)]
        .set(pair_ids)
    )
    source_rows = filler // top_count
    padded_tokens = jnp.concatenate([tokens, jnp.zeros((1, width_here), jnp.bfloat16)], axis=0)
    padded_cot = jnp.concatenate([cotangent, jnp.zeros((1, width_here), jnp.bfloat16)], axis=0)
    padded_gates = jnp.concatenate([gate_weights.reshape(-1), jnp.zeros((1,), jnp.float32)], axis=0)
    send_rows = padded_tokens[source_rows]
    send_cot = (padded_cot[source_rows].astype(jnp.float32) * padded_gates[filler][:, None]).astype(
        jnp.bfloat16
    )
    rows_in, cot_in = (
        lax.all_to_all(
            send_rows.reshape(groups, capacity, width_here),
            "expert",
            split_axis=0,
            concat_axis=0,
            tiled=True,
        ),
        lax.all_to_all(
            send_cot.reshape(groups, capacity, width_here),
            "expert",
            split_axis=0,
            concat_axis=0,
            tiled=True,
        ),
    )
    rows_in = rows_in.reshape(groups * capacity, width_here)
    cot_in = cot_in.reshape(groups * capacity, width_here)
    part_pre = contract_width(rows_in, gate_here)
    part_back = contract_width(cot_in, down_here)
    pre_sum, back_sum = (
        lax.psum(part_pre.astype(jnp.bfloat16), "hid").astype(jnp.float32),
        lax.psum(part_back.astype(jnp.bfloat16), "hid").astype(jnp.float32),
    )
    hidden, slope_rows = activate(pre_sum, back_sum)
    expert_out = jnp.dot(hidden, down_here, preferred_element_type=jnp.float32).astype(jnp.bfloat16)
    down_step = contract_rows(hidden, cot_in).astype(jnp.bfloat16)
    gate_step, back_rows = gate_side(slope_rows, rows_in, gate_here)
    spread = (
        lax.all_to_all(
            into_pieces(gate_step, groups), "expert", split_axis=0, concat_axis=0, tiled=True
        ),
        lax.all_to_all(
            into_pieces(down_step, groups), "expert", split_axis=0, concat_axis=0, tiled=True
        ),
    )
    placed = (
        lax.all_to_all(
            jnp.take(spread[0], source_of, axis=0),
            "expert",
            split_axis=0,
            concat_axis=0,
            tiled=True,
        ),
        lax.all_to_all(
            jnp.take(spread[1], source_of, axis=0),
            "expert",
            split_axis=0,
            concat_axis=0,
            tiled=True,
        ),
    )
    grad_gate = placed[0].reshape(gate_step.shape)
    grad_down = placed[1].reshape(down_step.shape)
    out_back, grads_back = (
        lax.all_to_all(
            expert_out.reshape(groups, capacity, width_here),
            "expert",
            split_axis=0,
            concat_axis=0,
            tiled=True,
        ),
        lax.all_to_all(
            back_rows.reshape(groups, capacity, width_here),
            "expert",
            split_axis=0,
            concat_axis=0,
            tiled=True,
        ),
    )
    out_flat = out_back.reshape(groups * capacity, width_here)
    grads_flat = grads_back.reshape(groups * capacity, width_here)
    picked_out = out_flat[position].astype(jnp.float32)
    layer_out = jnp.sum(picked_out * gate_weights[:, :, None], axis=1).astype(jnp.bfloat16)
    token_grads = jnp.sum(grads_flat[position].astype(jnp.float32), axis=1).astype(jnp.bfloat16)
    return (layer_out, token_grads, grad_gate[None], grad_down[None])


def solution(mesh):
    return jax.shard_map(
        per_device,
        mesh=mesh,
        in_specs=(
            P("expert", "hid"),
            P("expert", "hid"),
            P("expert", None),
            P("expert", None),
            P(),
            P(),
            P("expert", None, "hid"),
            P("expert", None, "hid"),
        ),
        out_specs=(
            P("expert", "hid"),
            P("expert", "hid"),
            P("expert", None, "hid"),
            P("expert", None, "hid"),
        ),
        check_vma=False,
    )
```

profile of v0, /device:TPU:8, one launch (start us, length us, event | category | flops | bytes accessed | tf_op | source)
XLA Modules:
  0.0 642.2 jit_solution(3986443375615933087)
XLA Ops:
  7.2 0.0 copy-start
  7.2 0.8 convert_reduce_fusion
  8.0 0.1 copy.17
  8.1 0.2 reduce_window_sum.11
  8.3 0.1 copy.19
  8.4 0.8 select_reduce_fusion.1
  9.2 0.1 copy.20
  9.3 0.1 add.80
  9.4 4.3 scatter_custom_fusion
  13.8 0.8 copy.22
  14.6 0.1 reshape.132
  14.7 0.0 copy-start.3
  14.7 7.1 %gather_fusion.3 = f32[1280]{0:T(1024)S(1)} fusion(f32[1025]{0:T(1024)S(1)} %pad_maximum_fusion, s32[2048]{0:T(1024)S(1)} %get-tuple-element.15), kind=kCustom, calls=%fused_computation.5 | custom fusion | bytes 15360 | tf_op jit(solution)/shard_map/gather | solution.py:68
  21.8 0.1 mul.87
  21.9 0.0 copy-done.3
  21.9 5.0 gather_fusion.2
  26.9 3.5 fusion.7
  30.4 0.0 copy-start.4
  30.4 10.8 %all-to-all-start.2 = ((bf16[32,40,896]{2,1,0:T(8,128)(2,1)}), bf16[32,40,896]{2,1,0:T(8,128)(2,1)}, u32[]{:S(2)}, u32[]{:S(2)}) async-start(bf16[32,40,896]{2,1,0:T(8,128)(2,1)} %fusion.7), calls=%async_computation.2 | async-start | bytes 4587520 | tf_op jit(solution)/shard_map/all_to_all | solution.py:79
  41.2 0.0 copy-done.4
  41.2 5.0 gather_fusion
  46.2 49.4 %all-to-all-done.2 = bf16[32,40,896]{2,1,0:T(8,128)(2,1)} async-done(((bf16[32,40,896]{2,1,0:T(8,128)(2,1)}), bf16[32,40,896]{2,1,0:T(8,128)(2,1)}, u32[]{:S(2)}, u32[]{:S(2)}) %all-to-all-start.2) | async-done | bytes 2293792 | tf_op jit(solution)/shard_map/all_to_all | solution.py:79
  95.6 6.3 all-to-all-start
  102.0 0.0 all-reduce.5.cloned.1.call-start
  102.0 6.6 %convolution_convert_fusion = bf16[1280,1024]{1,0:T(8,128)(2,1)} fusion(bf16[1280,896]{1,0:T(8,128)(2,1)} %bitcast.10, bf16[1,1024,896]{2,1,0:T(8,128)(2,1)} %param.17), kind=kOutput, calls=%fused_computation.20 | convolution fusion | flops 2350120960 | bytes 6750208 | tf_op jit(solution)/shard_map/dot_general | solution.py:12
  108.6 47.7 %all-to-all-done = bf16[32,40,896]{2,1,0:T(8,128)(2,1)} async-done(((bf16[32,40,896]{2,1,0:T(8,128)(2,1)}), bf16[32,40,896]{2,1,0:T(8,128)(2,1)}, u32[]{:S(2)}, u32[]{:S(2)}) %all-to-all-start) | async-done | bytes 2293792 | tf_op jit(solution)/shard_map/all_to_all | solution.py:72
  156.4 0.0 copy-done
  156.4 5.9 convolution_convert_fusion.1
  162.3 0.0 all-reduce.5.cloned.1.call-update
  162.3 128.3 %all-reduce.5.cloned.1.call-done = (bf16[1280,1024]{1,0:T(8,128)(2,1)}, bf16[1280,1024]{1,0:T(8,128)(2,1)}) async-done(((bf16[1280,1024]{1,0:T(8,128)(2,1)}, bf16[1280,1024]{1,0:T(8,128)(2,1)}), (bf16[1280,1024]{1,0:T(8,128)(2,1)}, bf16[1280,1024]{1,0:T(8,128)(2,1)})) %all-reduce.5.cloned.1.call-update) | async-done | bytes 5242896 | tf_op jit(solution)/shard_map/psum | solution.py:92
  290.6 3.9 fusion.6
  294.5 0.0 copy-start.2
  294.5 6.7 %convolution_convert_fusion.5 = bf16[1024,896]{1,0:T(8,128)(2,1)} fusion(bf16[1280,1024]{1,0:T(8,128)(2,1)S(1)} %fusion.6, bf16[1280,896]{1,0:T(8,128)(2,1)} %bitcast.2), kind=kOutput, calls=%fused_computation.34 | convolution fusion | flops 2349727744 | bytes 6750208 | tf_op jit(solution)/shard_map/dot_general | solution.py:18
  301.1 0.0 copy-done.2
  301.2 9.5 %all-to-all-start.4 = ((bf16[32,32,896]{2,1,0:T(8,128)(2,1)}), bf16[32,32,896]{2,1,0:T(8,128)(2,1)}, u32[]{:S(2)}, u32[]{:S(2)}) async-start(bf16[32,32,896]{2,1,0:T(8,128)(2,1)} %bitcast.45), calls=%async_computation.4 | async-start | bytes 3670016 | tf_op jit(solution)/shard_map/all_to_all | solution.py:100
  310.7 6.7 %convolution_convert_fusion.4 = bf16[1024,896]{1,0:T(8,128)(2,1)} fusion(bf16[1280,896]{1,0:T(8,128)(2,1)} %bitcast.10, bf16[1280,1024]{1,0:T(8,128)(2,1)} %get-tuple-element.7), kind=kOutput, calls=%fused_computation.33 | convolution fusion | flops 2357592064 | bytes 6750208 | tf_op jit(solution)/shard_map/dot_general | solution.py:18
  317.4 37.9 %all-to-all-done.4 = bf16[32,32,896]{2,1,0:T(8,128)(2,1)} async-done(((bf16[32,32,896]{2,1,0:T(8,128)(2,1)}), bf16[32,32,896]{2,1,0:T(8,128)(2,1)}, u32[]{:S(2)}, u32[]{:S(2)}) %all-to-all-start.4) | async-done | bytes 1835040 | tf_op jit(solution)/shard_map/all_to_all | solution.py:100
  355.3 6.1 all-to-all-start.6
  361.4 6.1 convolution_convert_fusion.2
  367.5 38.8 %all-to-all-done.6 = bf16[32,32,896]{2,1,0:T(8,128)(2,1)} async-done(((bf16[32,32,896]{2,1,0:T(8,128)(2,1)}), bf16[32,32,896]{2,1,0:T(8,128)(2,1)}, u32[]{:S(2)}, u32[]{:S(2)}) %all-to-all-start.6) | async-done | bytes 1835040 | tf_op jit(solution)/shard_map/all_to_all | solution.py:103
  406.3 6.0 all-to-all-start.3
  412.3 6.7 %convolution_convert_fusion.3 = bf16[1280,896]{1,0:T(8,128)(2,1)} fusion(bf16[1,1024,896]{2,1,0:T(8,128)(2,1)} %param.17, bf16[1280,1024]{1,0:T(8,128)(2,1)} %get-tuple-element.7), kind=kOutput, calls=%fused_computation.25 | convolution fusion | flops 2357821440 | bytes 6750208 | tf_op jit(solution)/shard_map/dot_general | solution.py:96
  419.0 47.7 %all-to-all-done.3 = bf16[32,40,896]{2,1,0:T(8,128)(2,1)} async-done(((bf16[32,40,896]{2,1,0:T(8,128)(2,1)}), bf16[32,40,896]{2,1,0:T(8,128)(2,1)}, u32[]{:S(2)}, u32[]{:S(2)}) %all-to-all-start.3) | async-done | bytes 2293792 | tf_op jit(solution)/shard_map/all_to_all | solution.py:133
  466.7 0.0 copy-start.5
  466.7 6.5 %all-to-all-start.1 = ((bf16[32,40,896]{2,1,0:T(8,128)(2,1)}), bf16[32,40,896]{2,1,0:T(8,128)(2,1)}, u32[]{:S(2)}, u32[]{:S(2)}) async-start(bf16[32,40,896]{2,1,0:T(8,128)(2,1)} %bitcast.42), calls=%async_computation.1 | async-start | bytes 4587520 | tf_op jit(solution)/shard_map/all_to_all | solution.py:126
  473.2 0.0 copy-done.5
  473.2 0.0 copy-done.6
  473.2 0.1 select_reduce_fusion.2
  473.3 3.5 gather_fusion.5
  476.8 3.5 gather_fusion.6
  480.3 4.3 broadcast_select_fusion
  484.6 43.0 %all-to-all-done.1 = bf16[32,40,896]{2,1,0:T(8,128)(2,1)} async-done(((bf16[32,40,896]{2,1,0:T(8,128)(2,1)}), bf16[32,40,896]{2,1,0:T(8,128)(2,1)}, u32[]{:S(2)}, u32[]{:S(2)}) %all-to-all-start.1) | async-done | bytes 2293792 | tf_op jit(solution)/shard_map/all_to_all | solution.py:126
  527.6 52.3 %all_to_all.40 = bf16[32,32,896]{2,1,0:T(8,128)(2,1)} all-to-all(bf16[32,32,896]{2,1,0:T(8,128)(2,1)} %get-tuple-element.14), channel_id=1, replica_groups=mesh['expert'=32,'hid'=8] {'expert'}, dimensions={0} | all-to-all | bytes 3670016 | tf_op jit(solution)/shard_map/all_to_all | solution.py:108
  579.9 5.2 all-to-all-start.7
  585.1 0.1 copy.21
  585.2 0.1 reshape.165
  585.3 7.7 %gather_fusion.4 = bf16[1024,896]{1,0:T(8,128)(2,1)} fusion(bf16[1280,896]{1,0:T(8,128)(2,1)} %bitcast.12, s32[1024]{0:T(1024)S(1)} %broadcast_clamp_fusion), kind=kCustom, calls=%fused_computation.6 | custom fusion | bytes 3674112 | tf_op jit(solution)/shard_map/gather | solution.py:145
  592.9 7.7 %gather_fusion.1 = bf16[1024,896]{1,0:T(8,128)(2,1)} fusion(bf16[1280,896]{1,0:T(8,128)(2,1)} %bitcast.6, s32[1024]{0:T(1024)S(1)} %broadcast_clamp_fusion), kind=kCustom, calls=%fused_computation.3 | custom fusion | bytes 3674112 | tf_op jit(solution)/shard_map/gather | solution.py:143
  600.6 3.5 bitcast_reduce_fusion
  604.2 0.0 copy-done.1
  604.2 1.9 fusion.8
  606.0 23.6 %all-to-all-done.7 = bf16[32,32,896]{2,1,0:T(8,128)(2,1)} async-done(((bf16[32,32,896]{2,1,0:T(8,128)(2,1)}), bf16[32,32,896]{2,1,0:T(8,128)(2,1)}, u32[]{:S(2)}, u32[]{:S(2)}) %all-to-all-start.7) | async-done | bytes 1835040 | tf_op jit(solution)/shard_map/all_to_all | solution.py:115
  629.6 2.9 copy.28
  632.5 2.9 copy.29
  (15 shorter events, 0.1 us)
Async XLA Ops:
  7.2 149.2 %copy-start = (bf16[1,1024,896]{2,1,0:T(8,128)(2,1)S(1)}, bf16[1,1024,896]{2,1,0:T(8,128)(2,1)}, u32[]{:S(2)}) copy-start(bf16[1,1024,896]{2,1,0:T(8,128)(2,1)} %param.16) | copy-start | bytes 5505028
  14.7 7.2 %copy-start.3 = (bf16[128,896]{1,0:T(8,128)(2,1)S(1)}, bf16[128,896]{1,0:T(8,128)(2,1)}, u32[]{:S(2)}) copy-start(bf16[128,896]{1,0:T(8,128)(2,1)} %param.11) | copy-start | bytes 688132
  30.4 10.8 %copy-start.4 = (bf16[128,896]{1,0:T(8,128)(2,1)S(1)}, bf16[128,896]{1,0:T(8,128)(2,1)}, u32[]{:S(2)}) copy-start(bf16[128,896]{1,0:T(8,128)(2,1)} %param.10) | copy-start | bytes 688132
  30.4 65.2 %all-to-all-start.2 = ((bf16[32,40,896]{2,1,0:T(8,128)(2,1)}), bf16[32,40,896]{2,1,0:T(8,128)(2,1)}, u32[]{:S(2)}, u32[]{:S(2)}) async-start(bf16[32,40,896]{2,1,0:T(8,128)(2,1)} %fusion.7), calls=%async_computation.2 | async-start | bytes 4587520 | tf_op jit(solution)/shard_map/all_to_all | solution.py:79
  95.6 60.8 %all-to-all-start = ((bf16[32,40,896]{2,1,0:T(8,128)(2,1)}), bf16[32,40,896]{2,1,0:T(8,128)(2,1)}, u32[]{:S(2)}, u32[]{:S(2)}) async-start(bf16[32,40,896]{2,1,0:T(8,128)(2,1)} %bitcast.39), calls=%async_computation | async-start | bytes 4587520 | tf_op jit(solution)/shard_map/all_to_all | solution.py:72
  102.0 188.6 %all-reduce.5.cloned.1.call-start = ((), (), s32[]{:S(2)}) async-start(), calls=%async_computation.8 | async-start | bytes 10485760 | tf_op jit(solution)/shard_map/psum | solution.py:92
  294.5 6.7 %copy-start.2 = (bf16[1280,1024]{1,0:T(8,128)(2,1)}, bf16[1280,1024]{1,0:T(8,128)(2,1)S(1)}, u32[]{:S(2)}) copy-start(bf16[1280,1024]{1,0:T(8,128)(2,1)S(1)} %fusion.6) | copy-start | bytes 7864324
  301.2 54.2 %all-to-all-start.4 = ((bf16[32,32,896]{2,1,0:T(8,128)(2,1)}), bf16[32,32,896]{2,1,0:T(8,128)(2,1)}, u32[]{:S(2)}, u32[]{:S(2)}) async-start(bf16[32,32,896]{2,1,0:T(8,128)(2,1)} %bitcast.45), calls=%async_computation.4 | async-start | bytes 3670016 | tf_op jit(solution)/shard_map/all_to_all | solution.py:100
  355.3 50.9 %all-to-all-start.6 = ((bf16[32,32,896]{2,1,0:T(8,128)(2,1)}), bf16[32,32,896]{2,1,0:T(8,128)(2,1)}, u32[]{:S(2)}, u32[]{:S(2)}) async-start(bf16[32,32,896]{2,1,0:T(8,128)(2,1)} %bitcast.44), calls=%async_computation.6 | async-start | bytes 3670016 | tf_op jit(solution)/shard_map/all_to_all | solution.py:103
  406.3 60.4 %all-to-all-start.3 = ((bf16[32,40,896]{2,1,0:T(8,128)(2,1)}), bf16[32,40,896]{2,1,0:T(8,128)(2,1)}, u32[]{:S(2)}, u32[]{:S(2)}) async-start(bf16[32,40,896]{2,1,0:T(8,128)(2,1)} %bitcast.43), calls=%async_computation.3 | async-start | bytes 4587520 | tf_op jit(solution)/shard_map/all_to_all | solution.py:133
  466.7 6.5 %copy-start.5 = (s32[32]{0:T(128)S(1)}, s32[32]{0:T(128)}, u32[]{:S(2)}) copy-start(s32[32]{0:T(128)} %param.14) | copy-start | bytes 388
  466.7 6.5 %copy-start.6 = (s32[32]{0:T(128)S(1)}, s32[32]{0:T(128)}, u32[]{:S(2)}) copy-start(s32[32]{0:T(128)} %param.15) | copy-start | bytes 388
  466.7 60.9 %all-to-all-start.1 = ((bf16[32,40,896]{2,1,0:T(8,128)(2,1)}), bf16[32,40,896]{2,1,0:T(8,128)(2,1)}, u32[]{:S(2)}, u32[]{:S(2)}) async-start(bf16[32,40,896]{2,1,0:T(8,128)(2,1)} %bitcast.42), calls=%async_computation.1 | async-start | bytes 4587520 | tf_op jit(solution)/shard_map/all_to_all | solution.py:126
  579.9 49.7 %all-to-all-start.7 = ((bf16[32,32,896]{2,1,0:T(8,128)(2,1)}), bf16[32,32,896]{2,1,0:T(8,128)(2,1)}, u32[]{:S(2)}, u32[]{:S(2)}) async-start(bf16[32,32,896]{2,1,0:T(8,128)(2,1)} %get-tuple-element.13), calls=%async_computation.7 | async-start | bytes 3670016 | tf_op jit(solution)/shard_map/all_to_all | solution.py:115
  600.6 3.5 copy-start.1
Sparse Core Ops, SparseCore 0:
  162.4 128.0 all-reduce.4
where the time goes:
time: 646 us; the launch traced here: 642 us
  waiting for transfers between devices  416 us (64%)
  blocking collectives  52.3 us (8%)
  local copies, waits for them, and re-layouts  51 us (8%)
  starting transfers between devices  50.5 us (8%)
  matrix products  38.7 us (6%)
  other arithmetic  19.1 us (3%)
  between operations  14.3 us (2%)
    psum x1, waiting for transfers between devices, per_device(): lax.psum(part_pre.astype(jnp.bfloat16), 'hid').astype(jnp.float32)  128 us
    all_to_all x1, blocking collectives, per_device(): lax.all_to_all(jnp.take(spread[0], source_of, axis=0), 'expert', split_ax...  52.3 us
    all_to_all x1, waiting for transfers between devices, per_device(): lax.all_to_all(send_cot.reshape(groups, capacity, width_here), 'expert',...  49.4 us
    all_to_all x1, waiting for transfers between devices, per_device(): lax.all_to_all(send_rows.reshape(groups, capacity, width_here), 'expert',...  47.7 us
    all_to_all x1, waiting for transfers between devices, per_device(): lax.all_to_all(back_rows.reshape(groups, capacity, width_here), 'expert',...  47.7 us
    all_to_all x1, waiting for transfers between devices, per_device(): lax.all_to_all(expert_out.reshape(groups, capacity, width_here), 'expert'...  43 us
    all_to_all x1, waiting for transfers between devices, per_device(): lax.all_to_all(into_pieces(down_step, groups), 'expert', split_axis=0, co...  38.8 us
    all_to_all x1, waiting for transfers between devices, per_device(): lax.all_to_all(into_pieces(gate_step, groups), 'expert', split_axis=0, co...  37.9 us
  transfers between devices with their start and end apart: 8, of which 8 were waited for; matrix products, arithmetic and copies ran while one was open for 10% of the time, Pallas kernels for 0%

commit v1 on v0

v1 whole, which is shorter than its diff:
```python
import functools

import jax
import jax.numpy as jnp
from jax import lax
from jax.experimental import pallas as pl
from jax.experimental.pallas import tpu as pltpu
from jax.sharding import PartitionSpec as P

MESH = pl.DeviceIdType.MESH
BF = jnp.bfloat16
F32 = jnp.float32
VMEM_LIMIT = 62 << 20
NZ, CAP, TOK, HALF, QUART = 8, 40, 128, 64, 32
ROWS, PAIR = 1280, 80


def place():
    e, d = lax.axis_index("expert"), lax.axis_index("hid")
    return e // 4, (e // 2) % 2, e % 2, d // 4, d % 4


class Links:
    def __init__(self, send_sem, recv_sem):
        self.z, self.h, self.c, self.lo, self.x = place()
        self.send_sem, self.recv_sem, self.used, self.sent = send_sem, recv_sem, 0, []

    def at(self, z=None, h=None, c=None, lo=None, x=None):
        z = self.z if z is None else z
        h = self.h if h is None else h
        c = self.c if c is None else c
        lo = self.lo if lo is None else lo
        x = self.x if x is None else x
        return (z * 4 + h * 2 + c, lo * 4 + x)

    def dz(self, k):
        return (self.z + k + NZ) % NZ

    def dx(self, k):
        return (self.x + k + 4) % 4

    def barrier(self):
        peers = [
            self.at(z=self.dz(1)),
            self.at(z=self.dz(-1)),
            self.at(h=1 - self.h),
            self.at(c=1 - self.c),
            self.at(x=self.dx(1)),
            self.at(x=self.dx(-1)),
            self.at(lo=1 - self.lo),
        ]
        sem = pltpu.get_barrier_semaphore()
        for peer in peers:
            pl.semaphore_signal(sem, inc=1, device_id=peer, device_id_type=MESH)
        pl.semaphore_wait(sem, len(peers))

    def new(self):
        self.used += 1
        return self.used - 1

    def send(self, src, dst, peer, sem=None):
        i = self.new()
        copy = pltpu.make_async_remote_copy(
            src_ref=src,
            dst_ref=dst,
            send_sem=self.send_sem.at[i],
            recv_sem=self.recv_sem.at[i if sem is None else sem],
            device_id=peer,
            device_id_type=MESH,
        )
        copy.start()
        self.sent.append(copy)
        return i

    def arrive(self, ref, i):
        pltpu.make_async_copy(ref, ref, self.recv_sem.at[i]).wait()

    def drain(self):
        for copy in self.sent:
            copy.wait_send()
        self.sent = []


def gather_flow(net, own, full, local_sem):
    z, h, c = net.z, net.h, net.c
    other_y, other_c = net.at(h=1 - h), net.at(c=1 - c)
    right, left = net.at(z=net.dz(1)), net.at(z=net.dz(-1))
    me = c * NZ + z
    ra, rb = pl.ds(0, HALF), pl.ds(HALF, HALF)
    a_first, a_last = pl.ds(0, QUART), pl.ds(QUART, QUART)
    b_first, b_last = pl.ds(HALF, QUART), pl.ds(HALF + QUART, QUART)
    core_sems = [net.new() for _ in range(NZ)]
    keep = pltpu.make_async_copy(own, full.at[me, h], local_sem)
    keep.start()
    ya = net.send(own.at[ra], full.at[me, h, ra], other_y)
    b_right = net.send(own.at[rb], full.at[me, h, rb], right)
    b_left = net.send(own.at[rb], full.at[me, h, rb], left)
    keep.wait()
    yb = [net.send(full.at[me, h, rb], full.at[me, h, rb], other_y)]

    def to_core(k, what):
        slot = c * NZ + net.dz(k)
        net.send(full.at[(slot,) + what], full.at[(slot,) + what], other_c, sem=core_sems[k % NZ])

    to_core(0, (h, slice(None)))
    both = slice(None)
    net.arrive(full.at[me, 1 - h, ra], ya)
    a_right = net.send(full.at[me, both, ra], full.at[me, both, ra], right)
    a_left = net.send(full.at[me, both, ra], full.at[me, both, ra], left)
    to_core(0, (1 - h, ra))
    yield
    pending = [(0, yb[0])]
    for k in range(4):
        zr, zl = c * NZ + net.dz(-1 - k), c * NZ + net.dz(1 + k)
        last, nxt_last = k == 3, k == 2
        br, bl = (b_first, b_last) if last else (rb, rb)
        net.arrive(full.at[zr, h, br], b_right)
        if not last:
            rows = b_first if nxt_last else rb
            b_right = net.send(full.at[zr, h, rows], full.at[zr, h, rows], right)
        net.arrive(full.at[zl, h, bl], b_left)
        if not last:
            rows = b_last if nxt_last else rb
            b_left = net.send(full.at[zl, h, rows], full.at[zl, h, rows], left)
        fresh = [(-1 - k, net.send(full.at[zr, h, rb], full.at[zr, h, rb], other_y))]
        to_core(-1 - k, (h, rb))
        if not last:
            fresh.append((1 + k, net.send(full.at[zl, h, rb], full.at[zl, h, rb], other_y)))
            to_core(1 + k, (h, rb))
        ar, al = (a_first, a_last) if last else (ra, ra)
        net.arrive(full.at[zr, both, ar], a_right)
        if not last:
            rows = a_first if nxt_last else ra
            a_right = net.send(full.at[zr, both, rows], full.at[zr, both, rows], right)
        net.arrive(full.at[zl, both, al], a_left)
        if not last:
            rows = a_last if nxt_last else ra
            a_left = net.send(full.at[zl, both, rows], full.at[zl, both, rows], left)
        to_core(-1 - k, (both, ra))
        if not last:
            to_core(1 + k, (both, ra))
        for d, sem in pending:
            slot = c * NZ + net.dz(d)
            net.arrive(full.at[slot, 1 - h, rb], sem)
            to_core(d, (1 - h, rb))
        pending = fresh
        yield
    for d, sem in pending:
        slot = c * NZ + net.dz(d)
        net.arrive(full.at[slot, 1 - h, rb], sem)
        to_core(d, (1 - h, rb))
    for k in range(NZ):
        net.arrive(full.at[(1 - c) * NZ + net.dz(k)], core_sems[k])
    yield


def small_gather(net, own, full, local_sem):
    z, h, c = net.z, net.h, net.c
    right, left = net.at(z=net.dz(1)), net.at(z=net.dz(-1))
    me = c * NZ + z
    keep = pltpu.make_async_copy(own, full.at[h, me], local_sem)
    keep.start()
    y = net.send(own, full.at[h, me], net.at(h=1 - h))
    keep.wait()
    net.arrive(full.at[1 - h, me], y)
    r = net.send(full.at[:, me], full.at[:, me], right)
    l = net.send(full.at[:, me], full.at[:, me], left)
    yield
    for k in range(4):
        zr, zl = c * NZ + net.dz(-1 - k), c * NZ + net.dz(1 + k)
        net.arrive(full.at[:, zr], r)
        if k < 3:
            r = net.send(full.at[:, zr], full.at[:, zr], right)
            net.arrive(full.at[:, zl], l)
            if k < 2:
                l = net.send(full.at[:, zl], full.at[:, zl], left)
        yield
    mine, theirs = pl.ds(pl.multiple_of(c * NZ, NZ), NZ), pl.ds(pl.multiple_of((1 - c) * NZ, NZ), NZ)
    i = net.send(full.at[:, mine], full.at[:, mine], net.at(c=1 - c))
    net.arrive(full.at[:, theirs], i)
    yield


def cols(xt, lo=None):
    if lo is None:
        return pl.ds(pl.multiple_of(xt * 256, 256), 256)
    return pl.ds(pl.multiple_of(xt * 256 + lo * 128, 128), 128)


def reduce_flow(net, part, out, hop_r, hop_l, in_r, in_l, y_out, y_in):
    x, lo = net.x, net.lo
    right, left = net.at(x=net.dx(1)), net.at(x=net.dx(-1))
    n = ROWS // 2
    r0, r1 = pl.ds(0, n), pl.ds(n, n)
    far, nr, nl, own = cols(net.dx(2)), cols(net.dx(1)), cols(net.dx(-1)), cols(x)
    s1 = net.send(part.at[r0, far], hop_r, right)
    s2 = net.send(part.at[r1, far], hop_l, left)
    yield
    s3 = net.send(part.at[r1, nr], in_r.at[r1], right)
    s4 = net.send(part.at[r0, nl], in_l.at[r0], left)
    yield
    tile = 160

    def add(dst_rows, where, src):
        def body(i, carry):
            at = pl.multiple_of(i * tile, tile)
            rows = pl.ds(pl.multiple_of(dst_rows + at, tile), tile)
            part[rows, where] = (
                part[rows, where].astype(F32) + src[pl.ds(at, tile), :].astype(F32)
            ).astype(BF)
            return carry

        lax.fori_loop(0, n // tile, body, 0)

    net.arrive(hop_r, s1)
    add(0, nr, hop_r)
    s5 = net.send(part.at[r0, nr], in_r.at[r0], right)
    net.arrive(hop_l, s2)
    add(n, nl, hop_l)
    s6 = net.send(part.at[r1, nl], in_l.at[r1], left)
    yield
    waits = {0: ((in_r, s5), (in_l, s4)), 1: ((in_r, s3), (in_l, s6))}
    ys = []
    for half in (1, 0):
        rows_half = (r0, r1)[half]
        for buf, sem in waits[half]:
            net.arrive(buf.at[rows_half], sem)

        def total(i, carry):
            rows = pl.ds(pl.multiple_of(half * n + i * tile, tile), tile)
            for side, keep in ((lo, True), (1 - lo, False)):
                inner = pl.ds(pl.multiple_of(side * 128, 128), 128)
                acc = (
                    part[rows, cols(x, side)].astype(F32)
                    + in_r[rows, inner].astype(F32)
                    + in_l[rows, inner].astype(F32)
                )
                if keep:
                    out[rows, :] = acc
                else:
                    y_out[rows, :] = acc.astype(BF)
            return carry

        lax.fori_loop(0, n // tile, total, 0)
        ys.append((half, net.send(y_out.at[rows_half], y_in.at[rows_half], net.at(lo=1 - lo))))
        yield
    for half, sem in ys:
        net.arrive(y_in.at[(r0, r1)[half]], sem)

        def last(i, carry):
            rows = pl.ds(pl.multiple_of(half * n + i * tile, tile), tile)
            out[rows, :] = out[rows, :] + y_in[rows, :].astype(F32)
            return carry

        lax.fori_loop(0, n // tile, last, 0)
    yield


def run_together(*flows):
    flows = list(flows)
    while flows:
        for flow in list(flows):
            try:
                next(flow)
            except StopIteration:
                flows.remove(flow)


def ranks(info, expert, tri, rank_ref, weight_ref):
    for side in range(2):
        hit = info[side, :, 0:8, :] == expert[...][0:1, :][None]
        mask = jnp.max(jnp.where(hit, 1.0, 0.0), axis=1)
        weight = jnp.sum(jnp.where(hit, info[side, :, 8:16, :], 0.0), axis=1)
        before = jnp.dot(mask.astype(BF), tri[...], preferred_element_type=F32)
        where = pl.ds(side * TOK, TOK)
        rank_ref[:, where] = jnp.where(mask > 0.5, before + float(side * CAP), -1.0)
        weight_ref[:, where] = weight


def picker(rank_ref, p):
    slots = lax.broadcasted_iota(jnp.int32, (PAIR, 2 * TOK), 0).astype(F32)
    return jnp.where(slots == rank_ref[pl.ds(p, 1), :], 1.0, 0.0)


def dispatch_kernel(
    tok, cot, info, wg, wd, eold, enew, tri,
    hid_o, slope_o, rows_new, cot_new,
    tok_all, cot_all, info_all, rows, part_a, part_b, acc_a, acc_b,
    hop_r, hop_l, in_r, in_l, y_out, y_in,
    rank_old, weight_old, rank_new, weight_new,
    local_sem, send_sem, recv_sem,
):
    net = Links(send_sem, recv_sem)
    net.barrier()
    small = small_gather(net, info, info_all, local_sem.at[0])
    toks = gather_flow(net, tok, tok_all, local_sem.at[1])
    cots = gather_flow(net, cot, cot_all, local_sem.at[2])
    run_together(small, toks)
    next(cots)
    ranks(info_all, eold, tri, rank_old, weight_old)
    ranks(info_all, enew, tri, rank_new, weight_new)
    next(cots)

    def pick_tok(p, carry):
        block = tok_all[p].reshape(2 * TOK, tok_all.shape[-1])
        at = pl.ds(pl.multiple_of(p * PAIR, 16), PAIR)
        for rank_ref, out in ((rank_old, rows), (rank_new, rows_new)):
            sel = picker(rank_ref, p).astype(BF)
            out[at, :] = jnp.dot(sel, block, preferred_element_type=F32).astype(BF)
        return carry

    def pick_cot(p, carry):
        block = cot_all[p].reshape(2 * TOK, cot_all.shape[-1])
        at = pl.ds(pl.multiple_of(p * PAIR, 16), PAIR)
        for rank_ref, weight_ref, out in ((rank_old, weight_old, rows), (rank_new, weight_new, cot_new)):
            hit = picker(rank_ref, p)
            weight = jnp.sum(hit * weight_ref[pl.ds(p, 1), :], axis=1, keepdims=True)
            sel = jnp.dot(hit.astype(BF), block, preferred_element_type=F32)
            out[at, :] = (sel * weight).astype(BF)
        return carry

    def project(w, part, shift):
        where = cols(net.dx(shift))
        tile = 320

        def body(i, carry):
            at = pl.ds(pl.multiple_of(i * tile, tile), tile)
            part[at, where] = lax.dot_general(
                rows[at, :], w[where, :], (((1,), (1,)), ((), ())), preferred_element_type=F32
            ).astype(BF)
            return carry

        lax.fori_loop(0, ROWS // tile, body, 0)

    def flow(w, part, out, bufs):
        project(w, part, 2)
        red = reduce_flow(net, part, out, *bufs)
        next(red)
        project(w, part, 1)
        project(w, part, -1)
        next(red)
        project(w, part, 0)
        yield
        yield from red

    bufs_a = [r.at[0] for r in (hop_r, hop_l, in_r, in_l, y_out, y_in)]
    bufs_b = [r.at[1] for r in (hop_r, hop_l, in_r, in_l, y_out, y_in)]
    lax.fori_loop(0, 16, pick_tok, 0)
    next(cots)
    run_together(flow(wg, part_a, acc_a, bufs_a), cots)
    lax.fori_loop(0, 16, pick_cot, 0)
    run_together(flow(wd, part_b, acc_b, bufs_b))

    def act(i, carry):
        at = pl.ds(pl.multiple_of(i * 160, 160), 160)
        pre, back = acc_a[at, :], acc_b[at, :]
        sig = jax.nn.sigmoid(pre)
        hid_o[at, :] = (pre * sig).astype(BF)
        slope_o[at, :] = (back * sig * (1.0 + pre * (1.0 - sig))).astype(BF)
        return carry

    lax.fori_loop(0, ROWS // 160, act, 0)
    net.drain()


def dispatch(tokens, cotangent, info, w_gate, w_down, eold, enew, tri):
    width = tokens.shape[1]
    vm = pl.BlockSpec(memory_space=pltpu.VMEM)
    sds = jax.ShapeDtypeStruct
    half = ROWS // 2
    return pl.pallas_call(
        dispatch_kernel,
        out_shape=(
            sds((ROWS, 128), BF),
            sds((ROWS, 128), BF),
            sds((ROWS, width), BF),
            sds((ROWS, width), BF),
        ),
        in_specs=[vm] * 8,
        out_specs=(vm,) * 4,
        scratch_shapes=[
            pltpu.VMEM((16, 2, TOK, width), BF),
            pltpu.VMEM((16, 2, TOK, width), BF),
            pltpu.VMEM((2, 16, 16, 128), F32),
            pltpu.VMEM((ROWS, width), BF),
            pltpu.VMEM((ROWS, 1024), BF),
            pltpu.VMEM((ROWS, 1024), BF),
            pltpu.VMEM((ROWS, 128), F32),
            pltpu.VMEM((ROWS, 128), F32),
            pltpu.VMEM((2, half, 256), BF),
            pltpu.VMEM((2, half, 256), BF),
            pltpu.VMEM((2, ROWS, 256), BF),
            pltpu.VMEM((2, ROWS, 256), BF),
            pltpu.VMEM((2, ROWS, 128), BF),
            pltpu.VMEM((2, ROWS, 128), BF),
            pltpu.VMEM((16, 256), F32),
            pltpu.VMEM((16, 256), F32),
            pltpu.VMEM((16, 256), F32),
            pltpu.VMEM((16, 256), F32),
            pltpu.SemaphoreType.DMA((3,)),
            pltpu.SemaphoreType.DMA((192,)),
            pltpu.SemaphoreType.DMA((192,)),
        ],
        compiler_params=pltpu.CompilerParams(
            collective_id=0, has_side_effects=True, vmem_limit_bytes=VMEM_LIMIT
        ),
    )(tokens, cotangent, info, w_gate, w_down, eold, enew, tri)


def contract_rows(left_mat, right_mat):
    return lax.dot_general(
        left_mat, right_mat, (((0,), (0,)), ((), ())), preferred_element_type=jnp.float32
    )


def exchange(a):
    return lax.all_to_all(a, "expert", split_axis=0, concat_axis=0, tiled=True)


def per_device(tokens, cotangent, expert_ids, gate_weights, owner_old, owner_new, w_gate, w_down):
    me = lax.axis_index("expert")
    labels = jnp.arange(32, dtype=jnp.int32)
    width = tokens.shape[1]
    info = jnp.concatenate([expert_ids.T.astype(F32), gate_weights.T], axis=0)
    eold = jnp.broadcast_to(jnp.sum(jnp.where(owner_old == me, labels, 0)).astype(F32), (8, 128))
    enew = jnp.broadcast_to(jnp.sum(jnp.where(owner_new == me, labels, 0)).astype(F32), (8, 128))
    lane = jnp.arange(128)
    tri = (lane[:, None] < lane[None, :]).astype(BF)
    gate_here, down_here = w_gate[0], w_down[0]
    hid_s, slope_s, rows_new, cot_new = dispatch(
        tokens, cotangent, info, gate_here, down_here, eold, enew, tri
    )

    def whole(shard):
        g = lax.all_gather(shard, "hid").reshape(2, 4, ROWS, 128)
        return g.transpose(2, 1, 0, 3).reshape(ROWS, 1024)

    moved_to = (owner_new[:, None] == labels[None, :]).astype(jnp.int32)
    source_of = jnp.sum(moved_to * owner_old[:, None], axis=0, dtype=jnp.int32)
    both = jnp.concatenate([hid_s, slope_s], axis=1).reshape(32, CAP, 256)
    moved = exchange(jnp.take(exchange(both), source_of, axis=0)).reshape(ROWS, 256)
    hidden, slope = whole(hid_s), whole(slope_s)
    hidden_new, slope_new = whole(moved[:, :128]), whole(moved[:, 128:])
    expert_out = jnp.dot(hidden, down_here, preferred_element_type=F32).astype(BF)
    back_rows = jnp.dot(slope, gate_here, preferred_element_type=F32).astype(BF)
    grad_gate = contract_rows(slope_new, rows_new).astype(BF)
    grad_down = contract_rows(hidden_new, cot_new).astype(BF)

    onehot = (expert_ids[:, :, None] == labels).astype(jnp.int32)
    per_token = jnp.sum(onehot, axis=1, dtype=jnp.int32)
    before = jnp.cumsum(per_token, axis=0, dtype=jnp.int32) - per_token
    slot_rank = jnp.sum(onehot * before[:, None, :], axis=2, dtype=jnp.int32)
    target = jnp.sum(onehot * owner_old, axis=2, dtype=jnp.int32)
    position = target * CAP + slot_rank

    def back(a):
        a = a.reshape(2, 8, 2, CAP, width).transpose(1, 2, 0, 3, 4).reshape(32, CAP, width)
        return exchange(a).reshape(ROWS, width)

    out_flat, grads_flat = back(expert_out), back(back_rows)
    picked_out = out_flat[position].astype(F32)
    layer_out = jnp.sum(picked_out * gate_weights[:, :, None], axis=1).astype(BF)
    token_grads = jnp.sum(grads_flat[position].astype(F32), axis=1).astype(BF)
    return (layer_out, token_grads, grad_gate[None], grad_down[None])


def solution(mesh):
    return jax.shard_map(
        per_device,
        mesh=mesh,
        in_specs=(
            P("expert", "hid"),
            P("expert", "hid"),
            P("expert", None),
            P("expert", None),
            P(),
            P(),
            P("expert", None, "hid"),
            P("expert", None, "hid"),
        ),
        out_specs=(
            P("expert", "hid"),
            P("expert", "hid"),
            P("expert", None, "hid"),
            P("expert", None, "hid"),
        ),
        check_vma=False,
    )
```

time: 646 us -> 402 us (0.62)
  waiting for transfers between devices: 416 us -> 137 us
  Pallas kernels: 0 us -> 140 us
  starting transfers between devices: 50.5 us -> 16.5 us
  blocking collectives: 52.3 us -> 25.6 us
  matrix products: 38.7 us -> 20.5 us
  local copies, waits for them, and re-layouts: 51 us -> 34.4 us
  other arithmetic: 19.1 us -> 10.2 us
    all_to_all x7 -> x3, waiting for transfers between devices: 288 us -> 39.8 us  [exchange(): return lax.all_to_all(a, 'expert', split_axis=0, concat_axis=0, tiled=True)]
    pallas_call x0 -> x1, Pallas kernels: none -> 140 us  [dispatch(): pl.pallas_call(dispatch_kernel, out_shape=(sds((ROWS, 128), BF), sds((ROW...]
    psum x1 -> x0, waiting for transfers between devices: 128 us -> none  [per_device(): lax.psum(part_pre.astype(jnp.bfloat16), 'hid').astype(jnp.float32)]
    all_gather x0 -> x4, waiting for transfers between devices: none -> 95.8 us  [whole(): g = lax.all_gather(shard, 'hid').reshape(2, 4, ROWS, 128)]
    all_to_all x7 -> x3, starting transfers between devices: 50.4 us -> 16.3 us  [exchange(): return lax.all_to_all(a, 'expert', split_axis=0, concat_axis=0, tiled=True)]
    gather x7 -> x3, local copies, waits for them, and re-layouts: 39.4 us -> 12.5 us  [the longest x1 6.6 us: per_device(): token_grads = jnp.sum(grads_flat[position].astype(F32), axis=1).astype(BF)]
    all_to_all x1, blocking collectives: 52.3 us -> 25.6 us  [exchange(): return lax.all_to_all(a, 'expert', split_axis=0, concat_axis=0, tiled=True)]
    dot_general x4 -> x2, matrix products: 25.3 us -> 9.86 us  [the longest x1 5.2 us: per_device(): back_rows = jnp.dot(slope, gate_here, preferred_element_type=F32).astype(BF)]
  transfers between devices with their start and end apart: 8 -> 7, of which waited for: 8 -> 5; matrix products, arithmetic and copies ran while one was open for 10% -> 12% of each run, Pallas kernels for 0% -> 0%
where the time goes in v1:
time: 402 us; the launch traced here: 399 us
  Pallas kernels  140 us (35%)
  waiting for transfers between devices  137 us (34%)
  local copies, waits for them, and re-layouts  34.4 us (9%)
  blocking collectives  25.6 us (6%)
  matrix products  20.5 us (5%)
  starting transfers between devices  16.5 us (4%)
  between operations  15.3 us (4%)
  other arithmetic  10.2 us (3%)
    pallas_call x1, Pallas kernels, dispatch(): pl.pallas_call(dispatch_kernel, out_shape=(sds((ROWS, 128), BF), sds((ROW...  140 us
    all_gather x4, waiting for transfers between devices, whole(): g = lax.all_gather(shard, 'hid').reshape(2, 4, ROWS, 128)  95.8 us
    all_to_all x3, waiting for transfers between devices, exchange(): return lax.all_to_all(a, 'expert', split_axis=0, concat_axis=0, tiled=True)  39.8 us
    all_to_all x1, blocking collectives, exchange(): return lax.all_to_all(a, 'expert', split_axis=0, concat_axis=0, tiled=True)  25.6 us
    all_to_all x3, starting transfers between devices, exchange(): return lax.all_to_all(a, 'expert', split_axis=0, concat_axis=0, tiled=True)  16.3 us
    dot_general x2, matrix products, contract_rows(): lax.dot_general(left_mat, right_mat, (((0,), (0,)), ((), ())), preferred_...  10.6 us
    transpose x2, local copies, waits for them, and re-layouts, whole(): return g.transpose(2, 1, 0, 3).reshape(ROWS, 1024)  8.78 us
  transfers between devices with their start and end apart: 7, of which 5 were waited for; matrix products, arithmetic and copies ran while one was open for 12% of the time, Pallas kernels for 0%

profile of v1, /device:TPU:8, one launch (start us, length us, event | category | flops | bytes accessed | tf_op | source)
XLA Modules:
  0.0 399.3 jit_solution(6102110568812288062)
XLA Ops:
  7.2 0.0 all-gather.9.cloned.1.call-start
  7.2 0.6 fusion.1.tri
  7.8 0.7 convert_bitcast_fusion.2
  8.5 1.3 fusion.2
  11.1 1.3 pad_maximum_fusion.1.info
  12.4 0.6 broadcast_in_dim.42.eold
  13.0 0.6 broadcast_in_dim.43.enew
  13.6 140.0 %shard_map.111 = (bf16[1280,128]{1,0:T(8,128)(2,1)}, bf16[1280,128]{1,0:T(8,128)(2,1)}, bf16[1280,896]{1,0:T(8,128)(2,1)}, bf16[1280,896]{1,0:T(8,128)(2,1)}) custom-call(bf16[128,896]{1,0:T(8,128)(2,1)} %tok.1, bf16[128,896]{1,0:T(8,128)(2,1)} %cot.1, f32[16,128]{1,0:T(8,128)} %pad_maximum_fusion.1.info, bf16[1024,896]{1,0:T(8,128)(2,1)} %bitcast.75, ...), custom_call_target="tpu_custom_call" | custom-call | tf_op jit(solution)/shard_map/pallas_call | solution.py:371
  153.6 0.0 copy-start.4
  153.6 0.0 copy-start.5
  153.6 0.0 all-gather.9.cloned.1.call-update
  153.6 0.0 all-gather.11.cloned.1.call-start
  153.7 0.7 all-gather.11.cloned.1.call-update
  154.4 2.0 pad_maximum_fusion
  156.4 5.3 %all-to-all-start.2 = ((bf16[32,40,256]{2,1,0:T(8,128)(2,1)}), bf16[32,40,256]{2,1,0:T(8,128)(2,1)S(1)}, u32[]{:S(2)}, u32[]{:S(2)}) async-start(bf16[32,40,256]{2,1,0:T(8,128)(2,1)} %bitcast.21), calls=%async_computation.2 | async-start | bytes 1310720 | tf_op jit(solution)/shard_map/all_to_all | solution.py:417
  161.7 0.0 all-gather.13.cloned.1.call-start
  161.8 0.0 copy-done.4
  161.8 0.0 copy-done.5
  161.8 0.1 select_reduce_fusion.2
  161.9 21.8 %all-to-all-done.2 = bf16[32,40,256]{2,1,0:T(8,128)(2,1)S(1)} async-done(((bf16[32,40,256]{2,1,0:T(8,128)(2,1)}), bf16[32,40,256]{2,1,0:T(8,128)(2,1)S(1)}, u32[]{:S(2)}, u32[]{:S(2)}) %all-to-all-start.2) | async-done | bytes 655392 | tf_op jit(solution)/shard_map/all_to_all | solution.py:417
  183.7 0.6 gather_fusion.2
  184.3 0.1 broadcast_select_fusion
  184.4 25.6 %all_to_all.20 = bf16[32,40,256]{2,1,0:T(8,128)(2,1)S(1)} all-to-all(bf16[32,40,256]{2,1,0:T(8,128)(2,1)S(1)} %broadcast_select_fusion), channel_id=1, replica_groups=mesh['expert'=32,'hid'=8] {'expert'}, dimensions={0} | all-to-all | bytes 1310720 | tf_op jit(solution)/shard_map/all_to_all | solution.py:417
  210.1 0.9 fusion.7
  211.0 0.0 all-gather.13.cloned.1.call-update
  211.0 0.0 all-gather.9.cloned.1.call-done
  211.0 3.0 copy.28
  214.0 4.7 %convolution_convert_fusion.1 = bf16[1280,896]{1,0:T(8,128)(2,1)S(1)} fusion(bf16[1280,1024]{0,1:T(8,128)(2,1)S(1)} %bitcast.69, bf16[1,1024,896]{2,1,0:T(8,128)(2,1)} %param.15), kind=kOutput, calls=%fused_computation.6 | convolution fusion | flops 2349957120 | bytes 6750208 | tf_op jit(solution)/shard_map/dot_general | solution.py:444
  218.7 1.5 copy.29
  220.2 4.9 %all-to-all-start = ((bf16[32,40,896]{2,1,0:T(8,128)(2,1)}), bf16[32,40,896]{2,1,0:T(8,128)(2,1)S(1)}, u32[]{:S(2)}, u32[]{:S(2)}) async-start(bf16[32,40,896]{2,1,0:T(8,128)(2,1)} %bitcast.62), calls=%async_computation | async-start | bytes 4587520 | tf_op jit(solution)/shard_map/all_to_all | solution.py:417
  225.1 0.0 all-gather.15.cloned.1.call-start
  225.1 0.5 all-gather.15.cloned.1.call-update
  225.7 29.0 %all-gather.11.cloned.1.call-done = bf16[10240,128]{1,0:T(8,128)(2,1)} async-done(((bf16[1280,128]{1,0:T(8,128)(2,1)}), bf16[10240,128]{1,0:T(8,128)(2,1)}) %all-gather.11.cloned.1.call-update) | async-done | bytes 2621456 | tf_op jit(solution)/shard_map/all_gather | solution.py:435
  254.7 4.4 %copy.35 = bf16[2,4,1280,128]{2,3,0,1:T(8,128)(2,1)} copy(bf16[2,4,1280,128]{3,2,1,0:T(8,128)(2,1)} %bitcast.64) | data formatting | bytes 5242880 | tf_op jit(solution)/shard_map/reshape | solution.py:435
  259.1 5.2 %convolution_convert_fusion = bf16[1280,896]{1,0:T(8,128)(2,1)S(1)} fusion(bf16[1280,1024]{0,1:T(8,128)(2,1)} %bitcast.70, bf16[1,1024,896]{2,1,0:T(8,128)(2,1)} %param.14), kind=kOutput, calls=%fused_computation.5 | convolution fusion | flops 2349957120 | bytes 6750208 | tf_op jit(solution)/shard_map/dot_general | solution.py:445
  264.3 1.6 copy.36
  265.9 18.0 %all-to-all-done = bf16[32,40,896]{2,1,0:T(8,128)(2,1)S(1)} async-done(((bf16[32,40,896]{2,1,0:T(8,128)(2,1)}), bf16[32,40,896]{2,1,0:T(8,128)(2,1)S(1)}, u32[]{:S(2)}, u32[]{:S(2)}) %all-to-all-start) | async-done | bytes 2293792 | tf_op jit(solution)/shard_map/all_to_all | solution.py:417
  283.9 0.0 copy-start.3
  284.0 0.0 copy-start.2
  284.0 6.1 %all-to-all-start.1 = ((bf16[32,40,896]{2,1,0:T(8,128)(2,1)}), bf16[32,40,896]{2,1,0:T(8,128)(2,1)}, u32[]{:S(2)}, u32[]{:S(2)}) async-start(bf16[32,40,896]{2,1,0:T(8,128)(2,1)} %bitcast.61), calls=%async_computation.1 | async-start | bytes 4587520 | tf_op jit(solution)/shard_map/all_to_all | solution.py:417
  290.1 0.0 copy-done.3
  290.1 0.1 copy.34
  290.2 0.0 copy-done.2
  290.2 0.1 copy.30
  290.3 0.2 reduce_window_sum.11
  290.5 0.1 copy.32
  290.6 0.1 select_reduce_fusion.1
  290.7 0.1 copy.33
  290.8 0.1 reshape.132
  290.9 16.5 %all-gather.13.cloned.1.call-done = bf16[10240,128]{1,0:T(8,128)(2,1)} async-done(((bf16[1280,128]{1,0:T(8,128)(2,1)}), bf16[10240,128]{1,0:T(8,128)(2,1)}) %all-gather.13.cloned.1.call-update) | async-done | bytes 2621456 | tf_op jit(solution)/shard_map/all_gather | solution.py:435
  307.4 4.4 %copy.37 = bf16[1280,4,2,128]{0,3,2,1:T(8,128)(2,1)} copy(bf16[1280,4,2,128]{3,0,1,2:T(8,128)(2,1)} %bitcast.63) | data formatting | bytes 5242880 | tf_op jit(solution)/shard_map/transpose | solution.py:436
  311.8 50.2 %all-gather.15.cloned.1.call-done = bf16[10240,128]{1,0:T(8,128)(2,1)} async-done(((bf16[1280,128]{1,0:T(8,128)(2,1)}), bf16[10240,128]{1,0:T(8,128)(2,1)}) %all-gather.15.cloned.1.call-update) | async-done | bytes 2621456 | tf_op jit(solution)/shard_map/all_gather | solution.py:435
  362.1 4.4 %copy.38 = bf16[1280,4,2,128]{0,3,2,1:T(8,128)(2,1)} copy(bf16[1280,4,2,128]{3,0,1,2:T(8,128)(2,1)} %bitcast.65) | data formatting | bytes 5242880 | tf_op jit(solution)/shard_map/transpose | solution.py:436
  366.4 6.7 %convert_bitcast_fusion.1 = bf16[1,1024,896]{2,1,0:T(8,128)(2,1)} fusion(bf16[1280,1024]{0,1:T(8,128)(2,1)} %bitcast.67, bf16[1280,896]{1,0:T(8,128)(2,1)} %get-tuple-element.10), kind=kOutput, calls=%fused_computation.9 | convolution fusion | flops 2349727744 | bytes 6750208 | tf_op jit(solution)/shard_map/dot_general | solution.py:411
  373.1 0.0 copy-done.1
  373.1 0.0 copy-done.6
  373.1 4.0 convert_bitcast_fusion
  377.1 5.3 %gather_fusion = bf16[1024,896]{1,0:T(8,128)(2,1)} fusion(bf16[1280,896]{1,0:T(8,128)(2,1)S(1)} %bitcast.60, s32[1024]{0:T(1024)S(1)} %broadcast_clamp_fusion), kind=kCustom, calls=%fused_computation | custom fusion | bytes 3674112 | tf_op jit(solution)/shard_map/gather | solution.py:461
  382.4 0.0 all-to-all-done.1
  382.4 6.6 %gather_fusion.1 = bf16[1024,896]{1,0:T(8,128)(2,1)S(1)} fusion(bf16[1280,896]{1,0:T(8,128)(2,1)} %bitcast.19, s32[1024]{0:T(1024)S(1)} %broadcast_clamp_fusion), kind=kCustom, calls=%fused_computation.1 | custom fusion | bytes 3674112 | tf_op jit(solution)/shard_map/gather | solution.py:463
  389.0 0.0 copy-start
  389.0 1.9 bitcast_reduce_fusion
  390.9 0.0 copy-done
  390.9 1.9 fusion
  (9 shorter events, 0.1 us)
Async XLA Ops:
  7.2 203.8 %all-gather.9.cloned.1.call-start = ((), (), s32[]{:S(2)}) async-start(), calls=%async_computation.4 | async-start | bytes 2949120 | tf_op jit(solution)/shard_map/all_gather | solution.py:435
  153.6 8.2 %copy-start.4 = (s32[32]{0:T(128)S(1)}, s32[32]{0:T(128)}, u32[]{:S(2)}) copy-start(s32[32]{0:T(128)} %param.12) | copy-start | bytes 388
  153.6 8.2 %copy-start.5 = (s32[32]{0:T(128)S(1)}, s32[32]{0:T(128)}, u32[]{:S(2)}) copy-start(s32[32]{0:T(128)} %param.13) | copy-start | bytes 388
  153.6 101.0 %all-gather.11.cloned.1.call-start = ((), (), s32[]{:S(2)}) async-start(), calls=%async_computation.5 | async-start | bytes 2949120 | tf_op jit(solution)/shard_map/all_gather | solution.py:435
  156.4 27.3 %all-to-all-start.2 = ((bf16[32,40,256]{2,1,0:T(8,128)(2,1)}), bf16[32,40,256]{2,1,0:T(8,128)(2,1)S(1)}, u32[]{:S(2)}, u32[]{:S(2)}) async-start(bf16[32,40,256]{2,1,0:T(8,128)(2,1)} %bitcast.21), calls=%async_computation.2 | async-start | bytes 1310720 | tf_op jit(solution)/shard_map/all_to_all | solution.py:417
  161.7 145.7 %all-gather.13.cloned.1.call-start = ((), (), s32[]{:S(2)}) async-start(), calls=%async_computation.6 | async-start | bytes 2949120 | tf_op jit(solution)/shard_map/all_gather | solution.py:435
  220.2 63.7 %all-to-all-start = ((bf16[32,40,896]{2,1,0:T(8,128)(2,1)}), bf16[32,40,896]{2,1,0:T(8,128)(2,1)S(1)}, u32[]{:S(2)}, u32[]{:S(2)}) async-start(bf16[32,40,896]{2,1,0:T(8,128)(2,1)} %bitcast.62), calls=%async_computation | async-start | bytes 4587520 | tf_op jit(solution)/shard_map/all_to_all | solution.py:417
  225.1 137.0 %all-gather.15.cloned.1.call-start = ((), (), s32[]{:S(2)}) async-start(), calls=%async_computation.7 | async-start | bytes 2949120 | tf_op jit(solution)/shard_map/all_gather | solution.py:435
  283.9 6.1 %copy-start.3 = (f32[128,8]{0,1:T(8,128)S(1)}, f32[128,8]{0,1:T(8,128)}, u32[]{:S(2)}) copy-start(f32[128,8]{0,1:T(8,128)} %param.11) | copy-start | bytes 12292
  284.0 6.2 %copy-start.2 = (s32[128,8]{0,1:T(8,128)S(1)}, s32[128,8]{0,1:T(8,128)}, u32[]{:S(2)}) copy-start(s32[128,8]{0,1:T(8,128)} %param.10) | copy-start | bytes 12292
  284.0 98.4 %all-to-all-start.1 = ((bf16[32,40,896]{2,1,0:T(8,128)(2,1)}), bf16[32,40,896]{2,1,0:T(8,128)(2,1)}, u32[]{:S(2)}, u32[]{:S(2)}) async-start(bf16[32,40,896]{2,1,0:T(8,128)(2,1)} %bitcast.61), calls=%async_computation.1 | async-start | bytes 4587520 | tf_op jit(solution)/shard_map/all_to_all | solution.py:417
  366.4 6.7 %copy-start.1 = (bf16[1280,4,2,128]{0,3,2,1:T(8,128)(2,1)S(1)}, bf16[1280,4,2,128]{0,3,2,1:T(8,128)(2,1)}, u32[]{:S(2)}) copy-start(bf16[1280,4,2,128]{0,3,2,1:T(8,128)(2,1)} %copy.38) | copy-start | bytes 7864324
  366.4 6.7 %copy-start.6 = (bf16[1280,896]{1,0:T(8,128)(2,1)S(1)}, bf16[1280,896]{1,0:T(8,128)(2,1)}, u32[]{:S(2)}) copy-start(bf16[1280,896]{1,0:T(8,128)(2,1)} %get-tuple-element.11) | copy-start | bytes 6881284
  389.0 1.9 copy-start
Sparse Core Ops, SparseCore 0:
  153.8 46.9 all-gather.8
  202.5 52.0 all-gather.10
  257.0 50.3 all-gather.12
  309.6 52.3 all-gather.14

commit v2 on v1

--- a/solution.py
+++ b/solution.py
@@ -39,10 +39,9 @@
     def dx(self, k):
         return (self.x + k + 4) % 4
 
-    def barrier(self):
-        peers = [
-            self.at(z=self.dz(1)),
-            self.at(z=self.dz(-1)),
+    def barrier(self, all_z=False):
+        peers = [self.at(z=self.dz(k)) for k in (range(1, NZ) if all_z else (1, -1))]
+        peers += [
             self.at(h=1 - self.h),
             self.at(c=1 - self.c),
             self.at(x=self.dx(1)),
@@ -284,10 +283,10 @@
 
 def dispatch_kernel(
     tok, cot, info, wg, wd, eold, enew, tri,
-    hid_o, slope_o, rows_new, cot_new,
+    hid_o, slope_o, rows_new, cot_new, rank_old, weight_old,
     tok_all, cot_all, info_all, rows, part_a, part_b, acc_a, acc_b,
     hop_r, hop_l, in_r, in_l, y_out, y_in,
-    rank_old, weight_old, rank_new, weight_new,
+    rank_new, weight_new,
     local_sem, send_sem, recv_sem,
 ):
     net = Links(send_sem, recv_sem)
@@ -375,9 +374,11 @@
             sds((ROWS, 128), BF),
             sds((ROWS, width), BF),
             sds((ROWS, width), BF),
+            sds((16, 256), F32),
+            sds((16, 256), F32),
         ),
         in_specs=[vm] * 8,
-        out_specs=(vm,) * 4,
+        out_specs=(vm,) * 6,
         scratch_shapes=[
             pltpu.VMEM((16, 2, TOK, width), BF),
             pltpu.VMEM((16, 2, TOK, width), BF),
@@ -395,8 +396,6 @@
             pltpu.VMEM((2, ROWS, 128), BF),
             pltpu.VMEM((16, 256), F32),
             pltpu.VMEM((16, 256), F32),
-            pltpu.VMEM((16, 256), F32),
-            pltpu.VMEM((16, 256), F32),
             pltpu.SemaphoreType.DMA((3,)),
             pltpu.SemaphoreType.DMA((192,)),
             pltpu.SemaphoreType.DMA((192,)),
@@ -407,60 +406,336 @@
     )(tokens, cotangent, info, w_gate, w_down, eold, enew, tri)
 
 
-def contract_rows(left_mat, right_mat):
-    return lax.dot_general(
-        left_mat, right_mat, (((0,), (0,)), ((), ())), preferred_element_type=jnp.float32
-    )
-
-
-def exchange(a):
-    return lax.all_to_all(a, "expert", split_axis=0, concat_axis=0, tiled=True)
+N1 = 704
+
+
+def whole_flow(net, own, full, local_sem):
+    x, lo = net.x, net.lo
+    right, left, other = net.at(x=net.dx(1)), net.at(x=net.dx(-1)), net.at(lo=1 - lo)
+    n2 = ROWS - N1
+    p, q = pl.ds(0, N1), pl.ds(N1, n2)
+    p0, p1 = pl.ds(0, N1 // 2), pl.ds(N1 // 2, N1 // 2)
+    q0, q1 = pl.ds(N1, n2 // 2), pl.ds(N1 + n2 // 2, n2 // 2)
+    mine = cols(x, lo)
+    keep = pltpu.make_async_copy(own, full.at[:, mine], local_sem)
+    keep.start()
+    y = net.send(own.at[p], full.at[p, mine], other)
+    qr = net.send(own.at[q], full.at[q, mine], right)
+    ql = net.send(own.at[q], full.at[q, mine], left)
+    ys = [(x, net.send(own.at[q], full.at[q, mine], other))]
+    keep.wait()
+    yield
+    net.arrive(full.at[p, cols(x, 1 - lo)], y)
+    pr = net.send(full.at[p, cols(x)], full.at[p, cols(x)], right)
+    pls = net.send(full.at[p, cols(x)], full.at[p, cols(x)], left)
+    yield
+    xl, xr, xf = net.dx(-1), net.dx(1), net.dx(2)
+
+    def fwd(rows, where, peer):
+        return net.send(full.at[rows, where], full.at[rows, where], peer)
+
+    net.arrive(full.at[q, cols(xl, lo)], qr)
+    q2r = fwd(q0, cols(xl, lo), right)
+    ys.append((xl, fwd(q, cols(xl, lo), other)))
+    net.arrive(full.at[q, cols(xr, lo)], ql)
+    q2l = fwd(q1, cols(xr, lo), left)
+    ys.append((xr, fwd(q, cols(xr, lo), other)))
+    yield
+    net.arrive(full.at[p, cols(xl)], pr)
+    p2r = fwd(p0, cols(xl), right)
+    net.arrive(full.at[p, cols(xr)], pls)
+    p2l = fwd(p1, cols(xr), left)
+    yield
+    net.arrive(full.at[q0, cols(xf, lo)], q2r)
+    net.arrive(full.at[q1, cols(xf, lo)], q2l)
+    ys.append((xf, fwd(q, cols(xf, lo), other)))
+    yield
+    net.arrive(full.at[p0, cols(xf)], p2r)
+    net.arrive(full.at[p1, cols(xf)], p2l)
+    for xt, sem in ys:
+        net.arrive(full.at[q, cols(xt, 1 - lo)], sem)
+    yield
+
+
+def move_flow(net, hid_s, slope_s, src_z, src_hc, spread, picked, moved, local_sems):
+    z, h, c = net.z, net.h, net.c
+    n = ROWS // NZ
+    hc = h * 2 + c
+    sems = []
+    keeps = []
+    for k in range(NZ):
+        zt = net.dz(k)
+        rows = pl.ds(pl.multiple_of(zt * n, n), n)
+        for m, src in enumerate((hid_s, slope_s)):
+            if k == 0:
+                copy = pltpu.make_async_copy(src.at[rows], spread.at[z, hc, m], local_sems.at[m])
+                copy.start()
+                keeps.append(copy)
+            else:
+                sems.append((-k, m, net.send(src.at[rows], spread.at[z, hc, m], net.at(z=zt))))
+    for copy in keeps:
+        copy.wait()
+    yield
+    for k, m, sem in sems:
+        net.arrive(spread.at[net.dz(k), hc, m], sem)
+    s = net.send(spread.at[:, hc], spread.at[:, hc], net.at(h=1 - h))
+    t = net.send(spread.at[:, hc], spread.at[:, hc], net.at(c=1 - c))
+    yield
+    net.arrive(spread.at[:, (1 - h) * 2 + c], s)
+    u = net.send(spread.at[:, (1 - h) * 2 + c], spread.at[:, (1 - h) * 2 + c], net.at(c=1 - c))
+    net.arrive(spread.at[:, h * 2 + 1 - c], t)
+    net.arrive(spread.at[:, (1 - h) * 2 + 1 - c], u)
+
+    def pick(i, carry):
+        picked[i] = spread[src_z[i], src_hc[i]]
+        return carry
+
+    lax.fori_loop(0, NZ, pick, 0)
+    yield
+    sems, keeps = [], []
+    mine = pl.ds(pl.multiple_of(z * n, n), n)
+    for k in range(NZ):
+        zt = net.dz(k)
+        for m in range(2):
+            if k == 0:
+                copy = pltpu.make_async_copy(picked.at[z, m], moved.at[m, mine], local_sems.at[m])
+                copy.start()
+                keeps.append(copy)
+            else:
+                sems.append((-k, m, net.send(picked.at[zt, m], moved.at[m, mine], net.at(z=zt))))
+    for copy in keeps:
+        copy.wait()
+    yield
+    for k, m, sem in sems:
+        net.arrive(moved.at[m, pl.ds(pl.multiple_of(net.dz(k) * n, n), n)], sem)
+    yield
+
+
+def add_into(dst, *srcs):
+    lead, rows = dst.shape[:-2], dst.shape[-2]
+
+    def body(i, carry):
+        at = pl.ds(pl.multiple_of(i * 16, 16), 16)
+        for j in range(lead[0] if lead else 1):
+            where = (j, at) if lead else (at,)
+            acc = dst[where].astype(F32)
+            for src in srcs:
+                acc = acc + src[where].astype(F32)
+            dst[where] = acc.astype(BF)
+        return carry
+
+    lax.fori_loop(0, rows // 16, body, 0)
+
+
+def return_flow(net, contribution, to_core, from_core, sums, y_b, ring_ra, ring_la, ring_rb, ring_lb, y_a, out):
+    z, h, c = net.z, net.h, net.c
+    width = out.shape[-1]
+    other_y, other_c = net.at(h=1 - h), net.at(c=1 - c)
+    right, left = net.at(z=net.dz(1)), net.at(z=net.dz(-1))
+    ra, rb = pl.ds(0, HALF), pl.ds(HALF, HALF)
+    a_first, a_last = pl.ds(0, QUART), pl.ds(QUART, QUART)
+    b_first, b_last = pl.ds(HALF, QUART), pl.ds(HALF + QUART, QUART)
+    both = slice(None)
+    core, yb = {}, {}
+    for k in (4, 3, -3, 2, -2, 1, -1, 0):
+        zt = net.dz(k)
+        to_core[zt] = contribution((1 - c) * NZ + zt).astype(BF).reshape(2, TOK, width)
+        core[k] = net.send(to_core.at[zt], from_core.at[zt], other_c)
+    yield
+    ar = al = br = bl = None
+    for s in range(5):
+        ks = (4,) if s == 0 else (0,) if s == 4 else (4 - s, s - 4)
+        for k in ks:
+            zt = net.dz(k)
+            net.arrive(from_core.at[zt], core[k])
+            got = from_core[zt].astype(F32).reshape(2 * TOK, width)
+            sums[zt] = (contribution(c * NZ + zt) + got).astype(BF).reshape(2, TOK, width)
+            yb[k] = net.send(sums.at[zt, 1 - h, rb], y_b.at[zt], other_y)
+        zr, zl = net.dz(4 - s), net.dz(s - 4)
+        if s == 0:
+            ar = net.send(sums.at[zr, both, a_first], ring_ra.at[0, both, a_first], right)
+            al = net.send(sums.at[zr, both, a_last], ring_la.at[0, both, a_last], left)
+            net.arrive(y_b.at[zr], yb[4])
+            add_into(sums.at[zr, h, rb], y_b.at[zr])
+            br = net.send(sums.at[zr, h, b_first], ring_rb.at[0, a_first], right)
+            bl = net.send(sums.at[zr, h, b_last], ring_lb.at[0, a_last], left)
+            yield
+            continue
+        at_r, at_l = (a_first, a_last) if s == 1 else (ra, ra)
+        bt_r, bt_l = (b_first, b_last) if s == 1 else (rb, rb)
+        if s < 4:
+            net.arrive(ring_ra.at[s - 1, both, at_r], ar)
+            add_into(sums.at[zr, both, at_r], ring_ra.at[s - 1, both, at_r])
+            ar = net.send(sums.at[zr, both, ra], ring_ra.at[s], right)
+            net.arrive(ring_la.at[s - 1, both, at_l], al)
+            add_into(sums.at[zl, both, at_l], ring_la.at[s - 1, both, at_l])
+            al = net.send(sums.at[zl, both, ra], ring_la.at[s], left)
+            for k in ks:
+                net.arrive(y_b.at[net.dz(k)], yb[k])
+                add_into(sums.at[net.dz(k), h, rb], y_b.at[net.dz(k)])
+            net.arrive(ring_rb.at[s - 1, at_r], br)
+            add_into(sums.at[zr, h, bt_r], ring_rb.at[s - 1, at_r])
+            br = net.send(sums.at[zr, h, rb], ring_rb.at[s], right)
+            net.arrive(ring_lb.at[s - 1, at_l], bl)
+            add_into(sums.at[zl, h, bt_l], ring_lb.at[s - 1, at_l])
+            bl = net.send(sums.at[zl, h, rb], ring_lb.at[s], left)
+            yield
+            continue
+        net.arrive(ring_ra.at[3], ar)
+        net.arrive(ring_la.at[3], al)
+        add_into(sums.at[z, both, ra], ring_ra.at[3], ring_la.at[3])
+        ya = net.send(sums.at[z, 1 - h, ra], y_a, other_y)
+        net.arrive(y_b.at[z], yb[0])
+        net.arrive(ring_rb.at[3], br)
+        net.arrive(ring_lb.at[3], bl)
+        out[rb, :] = (
+            sums[z, h, rb, :].astype(F32)
+            + y_b[z].astype(F32)
+            + ring_rb[3].astype(F32)
+            + ring_lb[3].astype(F32)
+        ).astype(BF)
+        yield
+        net.arrive(y_a, ya)
+        out[ra, :] = (sums[z, h, ra, :].astype(F32) + y_a[...].astype(F32)).astype(BF)
+    yield
+
+
+def finish_kernel(
+    hid_s, slope_s, rows_new, cot_new, rank, weight, wg, wd, src_z, src_hc,
+    layer_out, token_grads, grad_gate, grad_down,
+    hidden, slope, hidden_new, slope_new, spread, picked, moved, out_rows, back_rows,
+    to_core, from_core, sums, y_b, ring_ra, ring_la, ring_rb, ring_lb, y_a,
+    local_sem, send_sem, recv_sem,
+):
+    net = Links(send_sem, recv_sem)
+    net.barrier(all_z=True)
+    whole_h = whole_flow(net, hid_s, hidden, local_sem.at[0])
+    whole_s = whole_flow(net, slope_s, slope, local_sem.at[1])
+    move = move_flow(net, hid_s, slope_s, src_z, src_hc, spread, picked, moved, local_sem.at[pl.ds(2, 2)])
+
+    def weighted(i, carry):
+        at = pl.ds(pl.multiple_of(i * PAIR, 16), PAIR)
+        w = jnp.sum(picker(rank, i) * weight[pl.ds(i, 1), :], axis=1, keepdims=True)
+        out = jnp.dot(hidden[at, :], wd[...], preferred_element_type=F32)
+        out_rows[at, :] = (out * w).astype(BF)
+        return carry
+
+    def plain(i, carry):
+        at = pl.ds(pl.multiple_of(i * 160, 160), 160)
+        back_rows[at, :] = jnp.dot(slope[at, :], wg[...], preferred_element_type=F32).astype(BF)
+        return carry
+
+    def placed(rows):
+        def contribution(p):
+            sel = picker(rank, p).astype(BF)
+            at = pl.ds(pl.multiple_of(p * PAIR, 16), PAIR)
+            return lax.dot_general(sel, rows[at, :], (((0,), (0,)), ((), ())), preferred_element_type=F32)
+
+        return contribution
+
+    def outer(left, right, out):
+        def body(i, carry):
+            at = pl.ds(pl.multiple_of(i * 128, 128), 128)
+            out[at, :] = lax.dot_general(
+                left[:, at], right[...], (((0,), (0,)), ((), ())), preferred_element_type=F32
+            ).astype(BF)
+            return carry
+
+        lax.fori_loop(0, 8, body, 0)
+
+    bufs = (to_core, from_core, sums, y_b, ring_ra, ring_la, ring_rb, ring_lb, y_a)
+
+    def forward():
+        yield from whole_h
+        lax.fori_loop(0, 16, weighted, 0)
+        yield from return_flow(net, placed(out_rows), *[b.at[0] for b in bufs], layer_out)
+
+    def backward():
+        yield from whole_s
+        lax.fori_loop(0, ROWS // 160, plain, 0)
+        yield from return_flow(net, placed(back_rows), *[b.at[1] for b in bufs], token_grads)
+
+    def grads():
+        yield from move
+        first = whole_flow(net, moved.at[1], slope_new, local_sem.at[0])
+        second = whole_flow(net, moved.at[0], hidden_new, local_sem.at[1])
+        next(first)
+        next(second)
+        for _ in range(5):
+            next(first)
+            next(second)
+            yield
+        outer(slope_new, rows_new, grad_gate)
+        yield
+        outer(hidden_new, cot_new, grad_down)
+        yield
+
+    run_together(forward(), backward(), grads())
+    net.drain()
+
+
+def finish(*args):
+    width = args[2].shape[1]
+    vm = pl.BlockSpec(memory_space=pltpu.VMEM)
+    sm = pl.BlockSpec(memory_space=pltpu.SMEM)
+    sds = jax.ShapeDtypeStruct
+    n = ROWS // NZ
+    return pl.pallas_call(
+        finish_kernel,
+        out_shape=(
+            sds((TOK, width), BF),
+            sds((TOK, width), BF),
+            sds((1024, width), BF),
+            sds((1024, width), BF),
+        ),
+        in_specs=[vm] * 8 + [sm] * 2,
+        out_specs=(vm,) * 4,
+        scratch_shapes=[
+            pltpu.VMEM((ROWS, 1024), BF),
+            pltpu.VMEM((ROWS, 1024), BF),
+            pltpu.VMEM((ROWS, 1024), BF),
+            pltpu.VMEM((ROWS, 1024), BF),
+            pltpu.VMEM((NZ, 4, 2, n, 128), BF),
+            pltpu.VMEM((NZ, 2, n, 128), BF),
+            pltpu.VMEM((2, ROWS, 128), BF),
+            pltpu.VMEM((ROWS, width), BF),
+            pltpu.VMEM((ROWS, width), BF),
+            pltpu.VMEM((2, NZ, 2, TOK, width), BF),
+            pltpu.VMEM((2, NZ, 2, TOK, width), BF),
+            pltpu.VMEM((2, NZ, 2, TOK, width), BF),
+            pltpu.VMEM((2, NZ, HALF, width), BF),
+            pltpu.VMEM((2, 4, 2, HALF, width), BF),
+            pltpu.VMEM((2, 4, 2, HALF, width), BF),
+            pltpu.VMEM((2, 4, HALF, width), BF),
+            pltpu.VMEM((2, 4, HALF, width), BF),
+            pltpu.VMEM((2, HALF, width), BF),
+            pltpu.SemaphoreType.DMA((4,)),
+            pltpu.SemaphoreType.DMA((256,)),
+            pltpu.SemaphoreType.DMA((256,)),
+        ],
+        compiler_params=pltpu.CompilerParams(
+            collective_id=1, has_side_effects=True, vmem_limit_bytes=VMEM_LIMIT
+        ),
+    )(*args)
 
 
 def per_device(tokens, cotangent, expert_ids, gate_weights, owner_old, owner_new, w_gate, w_down):
     me = lax.axis_index("expert")
     labels = jnp.arange(32, dtype=jnp.int32)
-    width = tokens.shape[1]
     info = jnp.concatenate([expert_ids.T.astype(F32), gate_weights.T], axis=0)
     eold = jnp.broadcast_to(jnp.sum(jnp.where(owner_old == me, labels, 0)).astype(F32), (8, 128))
     enew = jnp.broadcast_to(jnp.sum(jnp.where(owner_new == me, labels, 0)).astype(F32), (8, 128))
     lane = jnp.arange(128)
     tri = (lane[:, None] < lane[None, :]).astype(BF)
+    targets = jnp.arange(NZ, dtype=jnp.int32) * 4 + me % 4
+    source = jnp.sum(jnp.where(owner_new[None, :] == targets[:, None], owner_old[None, :], 0), axis=1)
     gate_here, down_here = w_gate[0], w_down[0]
-    hid_s, slope_s, rows_new, cot_new = dispatch(
+    hid_s, slope_s, rows_new, cot_new, rank, weight = dispatch(
         tokens, cotangent, info, gate_here, down_here, eold, enew, tri
     )
-
-    def whole(shard):
-        g = lax.all_gather(shard, "hid").reshape(2, 4, ROWS, 128)
-        return g.transpose(2, 1, 0, 3).reshape(ROWS, 1024)
-
-    moved_to = (owner_new[:, None] == labels[None, :]).astype(jnp.int32)
-    source_of = jnp.sum(moved_to * owner_old[:, None], axis=0, dtype=jnp.int32)
-    both = jnp.concatenate([hid_s, slope_s], axis=1).reshape(32, CAP, 256)
-    moved = exchange(jnp.take(exchange(both), source_of, axis=0)).reshape(ROWS, 256)
-    hidden, slope = whole(hid_s), whole(slope_s)
-    hidden_new, slope_new = whole(moved[:, :128]), whole(moved[:, 128:])
-    expert_out = jnp.dot(hidden, down_here, preferred_element_type=F32).astype(BF)
-    back_rows = jnp.dot(slope, gate_here, preferred_element_type=F32).astype(BF)
-    grad_gate = contract_rows(slope_new, rows_new).astype(BF)
-    grad_down = contract_rows(hidden_new, cot_new).astype(BF)
-
-    onehot = (expert_ids[:, :, None] == labels).astype(jnp.int32)
-    per_token = jnp.sum(onehot, axis=1, dtype=jnp.int32)
-    before = jnp.cumsum(per_token, axis=0, dtype=jnp.int32) - per_token
-    slot_rank = jnp.sum(onehot * before[:, None, :], axis=2, dtype=jnp.int32)
-    target = jnp.sum(onehot * owner_old, axis=2, dtype=jnp.int32)
-    position = target * CAP + slot_rank
-
-    def back(a):
-        a = a.reshape(2, 8, 2, CAP, width).transpose(1, 2, 0, 3, 4).reshape(32, CAP, width)
-        return exchange(a).reshape(ROWS, width)
-
-    out_flat, grads_flat = back(expert_out), back(back_rows)
-    picked_out = out_flat[position].astype(F32)
-    layer_out = jnp.sum(picked_out * gate_weights[:, :, None], axis=1).astype(BF)
-    token_grads = jnp.sum(grads_flat[position].astype(F32), axis=1).astype(BF)
+    layer_out, token_grads, grad_gate, grad_down = finish(
+        hid_s, slope_s, rows_new, cot_new, rank, weight, gate_here, down_here, source // 4, source % 4
+    )
     return (layer_out, token_grads, grad_gate[None], grad_down[None])
 
 

time: 402 us -> 343 us (0.85)
  Pallas kernels: 140 us -> 325 us
  waiting for transfers between devices: 137 us -> 0 us
  local copies, waits for them, and re-layouts: 34.4 us -> 8.72 us
  blocking collectives: 25.6 us -> 0 us
  matrix products: 20.5 us -> 0 us
  starting transfers between devices: 16.5 us -> 0 us
  between operations: 15.3 us -> 1.97 us
  other arithmetic: 10.2 us -> 5.37 us
    pallas_call x0 -> x1, Pallas kernels: none -> 185 us  [finish(): pl.pallas_call(finish_kernel, out_shape=(sds((TOK, width), BF), sds((TOK,...]
    all_gather x4 -> x0, waiting for transfers between devices: 95.8 us -> none  [whole(): g = lax.all_gather(shard, 'hid').reshape(2, 4, ROWS, 128)]
    all_to_all x3 -> x0, waiting for transfers between devices: 39.8 us -> none  [exchange(): return lax.all_to_all(a, 'expert', split_axis=0, concat_axis=0, tiled=True)]
    all_to_all x1 -> x0, blocking collectives: 25.6 us -> none  [exchange(): return lax.all_to_all(a, 'expert', split_axis=0, concat_axis=0, tiled=True)]
    dot_general x4 -> x0, matrix products: 20.5 us -> none  [the longest x2 10.6 us: contract_rows(): lax.dot_general(left_mat, right_mat, (((0,), (0,)), ((), ())), preferred_...]
    all_to_all x3 -> x0, starting transfers between devices: 16.3 us -> none  [exchange(): return lax.all_to_all(a, 'expert', split_axis=0, concat_axis=0, tiled=True)]
    gather x3 -> x0, local copies, waits for them, and re-layouts: 12.5 us -> none  [the longest x1 6.6 us: per_device(): token_grads = jnp.sum(grads_flat[position].astype(F32), axis=1).astype(BF)]
    reshape x4 -> x0, local copies, waits for them, and re-layouts: 10.6 us -> none  [the longest x2 7.43 us: whole(): g = lax.all_gather(shard, 'hid').reshape(2, 4, ROWS, 128)]
  transfers between devices with their start and end apart: 7 -> 0, of which waited for: 5 -> 0; matrix products, arithmetic and copies ran while one was open for 12% -> 0% of each run, Pallas kernels for 0% -> 0%
where the time goes in v2:
time: 343 us; the launch traced here: 341 us
  Pallas kernels  325 us (95%)
  local copies, waits for them, and re-layouts  8.72 us (3%)
  other arithmetic  5.37 us (2%)
    pallas_call x1, Pallas kernels, finish(): pl.pallas_call(finish_kernel, out_shape=(sds((TOK, width), BF), sds((TOK,...  185 us
    pallas_call x1, Pallas kernels, dispatch(): pl.pallas_call(dispatch_kernel, out_shape=(sds((ROWS, 128), BF), sds((ROW...  140 us
    unnamed x6, local copies, waits for them, and re-layouts  7.53 us

profile of v2, /device:TPU:8, one launch (start us, length us, event | category | flops | bytes accessed | tf_op | source)
XLA Modules:
  0.0 341.3 jit_solution(9778321662529869408)
XLA Ops:
  0.7 0.9 select_reduce_fusion
  1.5 0.6 and_select_fusion
  2.1 1.3 fusion.1
  4.7 0.6 broadcast_in_dim.35.eold
  5.3 0.6 broadcast_in_dim.36.enew
  5.9 0.7 convert_bitcast_fusion
  6.6 1.3 pad_maximum_fusion.info
  7.9 0.6 fusion.tri
  8.5 139.9 %shard_map.111 = (bf16[1280,128]{1,0:T(8,128)(2,1)}, bf16[1280,128]{1,0:T(8,128)(2,1)}, bf16[1280,896]{1,0:T(8,128)(2,1)}, bf16[1280,896]{1,0:T(8,128)(2,1)}, f32[16,256]{1,0:T(8,128)}, /*index=5*/f32[16,256]{1,0:T(8,128)}) custom-call(bf16[128,896]{1,0:T(8,128)(2,1)} %tok.1, bf16[128,896]{1,0:T(8,128)(2,1)} %cot.1, f32[16,128]{1,0:T(8,128)} %pad_maximum_fusion.info, ...), custom_call_target="tpu_custom_call" | custom-call | tf_op jit(solution)/shard_map/pallas_call | solution.py:370
  148.4 185.3 %shard_map.112 = (bf16[128,896]{1,0:T(8,128)(2,1)}, bf16[128,896]{1,0:T(8,128)(2,1)}, bf16[1024,896]{1,0:T(8,128)(2,1)}, bf16[1024,896]{1,0:T(8,128)(2,1)}) custom-call(bf16[1280,128]{1,0:T(8,128)(2,1)} %get-tuple-element.14.hid_s, bf16[1280,128]{1,0:T(8,128)(2,1)} %get-tuple-element.15.slope_s, bf16[1280,896]{1,0:T(8,128)(2,1)} %get-tuple-element.16.rows_new, ...), custom_call_target="tpu_custom_call" | custom-call | tf_op jit(solution)/shard_map/pallas_call | solution.py:683
  333.8 1.6 copy.16
  335.4 1.6 copy.17
  337.0 0.0 copy-start
  337.0 3.0 copy.18
  340.1 0.0 copy-done
  340.1 1.2 copy.19
  (1 shorter events, 0.0 us)
Async XLA Ops:
  337.0 3.0 copy-start

commit v3 on v2

--- a/solution.py
+++ b/solution.py
@@ -39,8 +39,8 @@
     def dx(self, k):
         return (self.x + k + 4) % 4
 
-    def barrier(self, all_z=False):
-        peers = [self.at(z=self.dz(k)) for k in (range(1, NZ) if all_z else (1, -1))]
+    def barrier(self):
+        peers = [self.at(z=self.dz(k)) for k in range(1, NZ)]
         peers += [
             self.at(h=1 - self.h),
             self.at(c=1 - self.c),
@@ -252,10 +252,9 @@
             return carry
 
         lax.fori_loop(0, n // tile, last, 0)
-    yield
-
-
-def run_together(*flows):
+
+
+def together(*flows):
     flows = list(flows)
     while flows:
         for flow in list(flows):
@@ -263,14 +262,117 @@
                 next(flow)
             except StopIteration:
                 flows.remove(flow)
-
-
-def ranks(info, expert, tri, rank_ref, weight_ref):
+        yield
+
+
+def run_together(*flows):
+    for _ in together(*flows):
+        pass
+
+
+def later(turns, flow):
+    for _ in range(turns):
+        yield
+    yield from flow
+
+
+def whole_flow(net, own, full, local_sem):
+    x, lo = net.x, net.lo
+    n = ROWS // 2
+    right, left, other = net.at(x=net.dx(1)), net.at(x=net.dx(-1)), net.at(lo=1 - lo)
+    h0, h1, rows = pl.ds(0, n), pl.ds(n, n), (pl.ds(0, n), pl.ds(n, n))
+    mine = cols(x, lo)
+    keep = pltpu.make_async_copy(own, full.at[:, mine], local_sem)
+    keep.start()
+    ys = [net.send(own.at[r], full.at[r, mine], other) for r in rows]
+    keep.wait()
+    yield
+
+    def fwd(r, where, peer):
+        return net.send(full.at[r, where], full.at[r, where], peer)
+
+    one_r, one_l = [], []
+    for r, y in zip(rows, ys):
+        net.arrive(full.at[r, cols(x, 1 - lo)], y)
+        one_r.append(fwd(r, cols(x), right))
+        one_l.append(fwd(r, cols(x), left))
+    yield
+    xl, xr, xf = net.dx(-1), net.dx(1), net.dx(2)
+    net.arrive(full.at[h0, cols(xl)], one_r[0])
+    two_r = fwd(h0, cols(xl), right)
+    net.arrive(full.at[h0, cols(xr)], one_l[0])
+    yield
+    net.arrive(full.at[h1, cols(xr)], one_l[1])
+    two_l = fwd(h1, cols(xr), left)
+    net.arrive(full.at[h1, cols(xl)], one_r[1])
+    yield
+    net.arrive(full.at[h0, cols(xf)], two_r)
+    net.arrive(full.at[h1, cols(xf)], two_l)
+    yield
+
+
+def look_up(table, wanted, value):
+    found = jnp.int32(0)
+    for i in range(32):
+        found = found + jnp.where(table[i] == wanted, value(i), 0)
+    return found
+
+
+def move_flow(net, shard, old, new, spread, picked, moved, local_sem):
+    z, h, c = net.z, net.h, net.c
+    n = ROWS // NZ
+    hc, yc = h * 2 + c, (1 - h) * 2 + c
+    far_first = (4, 3, -3, 2, -2, 1, -1)
+
+    def eighth(zt):
+        return pl.ds(pl.multiple_of(zt * n, n), n)
+
+    keep = pltpu.make_async_copy(shard.at[eighth(z)], spread.at[z, hc], local_sem)
+    keep.start()
+    sems = []
+    for k in far_first:
+        zt = net.dz(k)
+        sems.append((-k, net.send(shard.at[eighth(zt)], spread.at[z, hc], net.at(z=zt))))
+    keep.wait()
+    yield
+    for k, sem in sems:
+        net.arrive(spread.at[net.dz(k), hc], sem)
+    s = net.send(spread.at[:, hc], spread.at[:, hc], net.at(h=1 - h))
+    t = net.send(spread.at[:, hc], spread.at[:, hc], net.at(c=1 - c))
+    yield
+    net.arrive(spread.at[:, yc], s)
+    u = net.send(spread.at[:, yc], spread.at[:, yc], net.at(c=1 - c))
+    net.arrive(spread.at[:, h * 2 + 1 - c], t)
+    net.arrive(spread.at[:, (1 - h) * 2 + 1 - c], u)
+
+    def pick(i, carry):
+        source = look_up(new, i * 4 + hc, lambda e: old[e])
+        picked[i] = spread[source // 4, source % 4]
+        return carry
+
+    lax.fori_loop(0, NZ, pick, 0)
+    keep = pltpu.make_async_copy(picked.at[z], moved.at[eighth(z)], local_sem)
+    keep.start()
+    sems = []
+    for k in far_first:
+        zt = net.dz(k)
+        sems.append((-k, net.send(picked.at[zt], moved.at[eighth(z)], net.at(z=zt))))
+    keep.wait()
+    yield
+    for k, sem in sems:
+        net.arrive(moved.at[eighth(net.dz(k))], sem)
+    yield
+
+
+def ranks(info, expert, rank_ref, weight_ref):
+    expert = expert.astype(F32)
+    row = lax.broadcasted_iota(jnp.int32, (TOK, TOK), 0)
+    tri = jnp.where(row < lax.broadcasted_iota(jnp.int32, (TOK, TOK), 1), 1.0, 0.0).astype(BF)
     for side in range(2):
-        hit = info[side, :, 0:8, :] == expert[...][0:1, :][None]
+        hit = info[side, :, 0:8, :] == expert
         mask = jnp.max(jnp.where(hit, 1.0, 0.0), axis=1)
         weight = jnp.sum(jnp.where(hit, info[side, :, 8:16, :], 0.0), axis=1)
-        before = jnp.dot(mask.astype(BF), tri[...], preferred_element_type=F32)
+        before = jnp.dot(mask.astype(BF), tri, preferred_element_type=F32)
         where = pl.ds(side * TOK, TOK)
         rank_ref[:, where] = jnp.where(mask > 0.5, before + float(side * CAP), -1.0)
         weight_ref[:, where] = weight
@@ -282,23 +384,24 @@
 
 
 def dispatch_kernel(
-    tok, cot, info, wg, wd, eold, enew, tri,
-    hid_o, slope_o, rows_new, cot_new, rank_old, weight_old,
+    tok, cot, info, wg, wd, old, new,
+    slope_o, hidden, hid_moved, rows_new, cot_new, rank_old, weight_old,
     tok_all, cot_all, info_all, rows, part_a, part_b, acc_a, acc_b,
     hop_r, hop_l, in_r, in_l, y_out, y_in,
-    rank_new, weight_new,
+    rank_new, weight_new, hid_s, spread, picked,
     local_sem, send_sem, recv_sem,
 ):
     net = Links(send_sem, recv_sem)
     net.barrier()
     small = small_gather(net, info, info_all, local_sem.at[0])
     toks = gather_flow(net, tok, tok_all, local_sem.at[1])
-    cots = gather_flow(net, cot, cot_all, local_sem.at[2])
-    run_together(small, toks)
-    next(cots)
-    ranks(info_all, eold, tri, rank_old, weight_old)
-    ranks(info_all, enew, tri, rank_new, weight_new)
-    next(cots)
+    cots = later(2, gather_flow(net, cot, cot_all, local_sem.at[2]))
+    for turn, _ in enumerate(together(small, toks)):
+        if turn < 6:
+            next(cots)
+    me = net.z * 4 + net.h * 2 + net.c
+    ranks(info_all, look_up(old, me, jnp.int32), rank_old, weight_old)
+    ranks(info_all, look_up(new, me, jnp.int32), rank_new, weight_new)
 
     def pick_tok(p, carry):
         block = tok_all[p].reshape(2 * TOK, tok_all.shape[-1])
@@ -344,41 +447,57 @@
 
     bufs_a = [r.at[0] for r in (hop_r, hop_l, in_r, in_l, y_out, y_in)]
     bufs_b = [r.at[1] for r in (hop_r, hop_l, in_r, in_l, y_out, y_in)]
-    lax.fori_loop(0, 16, pick_tok, 0)
-    next(cots)
-    run_together(flow(wg, part_a, acc_a, bufs_a), cots)
-    lax.fori_loop(0, 16, pick_cot, 0)
-    run_together(flow(wd, part_b, acc_b, bufs_b))
-
-    def act(i, carry):
+    def act_hidden(i, carry):
+        at = pl.ds(pl.multiple_of(i * 160, 160), 160)
+        pre = acc_a[at, :]
+        hid_s[at, :] = (pre * jax.nn.sigmoid(pre)).astype(BF)
+        return carry
+
+    def act_slope(i, carry):
         at = pl.ds(pl.multiple_of(i * 160, 160), 160)
         pre, back = acc_a[at, :], acc_b[at, :]
         sig = jax.nn.sigmoid(pre)
-        hid_o[at, :] = (pre * sig).astype(BF)
         slope_o[at, :] = (back * sig * (1.0 + pre * (1.0 - sig))).astype(BF)
         return carry
 
-    lax.fori_loop(0, ROWS // 160, act, 0)
+    def pre_path():
+        lax.fori_loop(0, 16, pick_tok, 0)
+        yield from flow(wg, part_a, acc_a, bufs_a)
+        lax.fori_loop(0, ROWS // 160, act_hidden, 0)
+        yield from together(
+            whole_flow(net, hid_s, hidden, local_sem.at[1]),
+            move_flow(net, hid_s, old, new, spread, picked, hid_moved, local_sem.at[2]),
+        )
+
+    def back_path():
+        yield from cots
+        lax.fori_loop(0, 16, pick_cot, 0)
+        yield from flow(wd, part_b, acc_b, bufs_b)
+
+    run_together(pre_path(), back_path())
+    lax.fori_loop(0, ROWS // 160, act_slope, 0)
     net.drain()
 
 
-def dispatch(tokens, cotangent, info, w_gate, w_down, eold, enew, tri):
-    width = tokens.shape[1]
+def dispatch(*args):
+    width = args[0].shape[1]
     vm = pl.BlockSpec(memory_space=pltpu.VMEM)
+    sm = pl.BlockSpec(memory_space=pltpu.SMEM)
     sds = jax.ShapeDtypeStruct
     half = ROWS // 2
     return pl.pallas_call(
         dispatch_kernel,
         out_shape=(
             sds((ROWS, 128), BF),
+            sds((ROWS, 1024), BF),
             sds((ROWS, 128), BF),
             sds((ROWS, width), BF),
             sds((ROWS, width), BF),
             sds((16, 256), F32),
             sds((16, 256), F32),
         ),
-        in_specs=[vm] * 8,
-        out_specs=(vm,) * 6,
+        in_specs=[vm] * 5 + [sm] * 2,
+        out_specs=(vm,) * 7,
         scratch_shapes=[
             pltpu.VMEM((16, 2, TOK, width), BF),
             pltpu.VMEM((16, 2, TOK, width), BF),
@@ -396,119 +515,17 @@
             pltpu.VMEM((2, ROWS, 128), BF),
             pltpu.VMEM((16, 256), F32),
             pltpu.VMEM((16, 256), F32),
+            pltpu.VMEM((ROWS, 128), BF),
+            pltpu.VMEM((NZ, 4, ROWS // NZ, 128), BF),
+            pltpu.VMEM((NZ, ROWS // NZ, 128), BF),
             pltpu.SemaphoreType.DMA((3,)),
-            pltpu.SemaphoreType.DMA((192,)),
-            pltpu.SemaphoreType.DMA((192,)),
+            pltpu.SemaphoreType.DMA((256,)),
+            pltpu.SemaphoreType.DMA((256,)),
         ],
         compiler_params=pltpu.CompilerParams(
             collective_id=0, has_side_effects=True, vmem_limit_bytes=VMEM_LIMIT
         ),
-    )(tokens, cotangent, info, w_gate, w_down, eold, enew, tri)
-
-
-N1 = 704
-
-
-def whole_flow(net, own, full, local_sem):
-    x, lo = net.x, net.lo
-    right, left, other = net.at(x=net.dx(1)), net.at(x=net.dx(-1)), net.at(lo=1 - lo)
-    n2 = ROWS - N1
-    p, q = pl.ds(0, N1), pl.ds(N1, n2)
-    p0, p1 = pl.ds(0, N1 // 2), pl.ds(N1 // 2, N1 // 2)
-    q0, q1 = pl.ds(N1, n2 // 2), pl.ds(N1 + n2 // 2, n2 // 2)
-    mine = cols(x, lo)
-    keep = pltpu.make_async_copy(own, full.at[:, mine], local_sem)
-    keep.start()
-    y = net.send(own.at[p], full.at[p, mine], other)
-    qr = net.send(own.at[q], full.at[q, mine], right)
-    ql = net.send(own.at[q], full.at[q, mine], left)
-    ys = [(x, net.send(own.at[q], full.at[q, mine], other))]
-    keep.wait()
-    yield
-    net.arrive(full.at[p, cols(x, 1 - lo)], y)
-    pr = net.send(full.at[p, cols(x)], full.at[p, cols(x)], right)
-    pls = net.send(full.at[p, cols(x)], full.at[p, cols(x)], left)
-    yield
-    xl, xr, xf = net.dx(-1), net.dx(1), net.dx(2)
-
-    def fwd(rows, where, peer):
-        return net.send(full.at[rows, where], full.at[rows, where], peer)
-
-    net.arrive(full.at[q, cols(xl, lo)], qr)
-    q2r = fwd(q0, cols(xl, lo), right)
-    ys.append((xl, fwd(q, cols(xl, lo), other)))
-    net.arrive(full.at[q, cols(xr, lo)], ql)
-    q2l = fwd(q1, cols(xr, lo), left)
-    ys.append((xr, fwd(q, cols(xr, lo), other)))
-    yield
-    net.arrive(full.at[p, cols(xl)], pr)
-    p2r = fwd(p0, cols(xl), right)
-    net.arrive(full.at[p, cols(xr)], pls)
-    p2l = fwd(p1, cols(xr), left)
-    yield
-    net.arrive(full.at[q0, cols(xf, lo)], q2r)
-    net.arrive(full.at[q1, cols(xf, lo)], q2l)
-    ys.append((xf, fwd(q, cols(xf, lo), other)))
-    yield
-    net.arrive(full.at[p0, cols(xf)], p2r)
-    net.arrive(full.at[p1, cols(xf)], p2l)
-    for xt, sem in ys:
-        net.arrive(full.at[q, cols(xt, 1 - lo)], sem)
-    yield
-
-
-def move_flow(net, hid_s, slope_s, src_z, src_hc, spread, picked, moved, local_sems):
-    z, h, c = net.z, net.h, net.c
-    n = ROWS // NZ
-    hc = h * 2 + c
-    sems = []
-    keeps = []
-    for k in range(NZ):
-        zt = net.dz(k)
-        rows = pl.ds(pl.multiple_of(zt * n, n), n)
-        for m, src in enumerate((hid_s, slope_s)):
-            if k == 0:
-                copy = pltpu.make_async_copy(src.at[rows], spread.at[z, hc, m], local_sems.at[m])
-                copy.start()
-                keeps.append(copy)
-            else:
-                sems.append((-k, m, net.send(src.at[rows], spread.at[z, hc, m], net.at(z=zt))))
-    for copy in keeps:
-        copy.wait()
-    yield
-    for k, m, sem in sems:
-        net.arrive(spread.at[net.dz(k), hc, m], sem)
-    s = net.send(spread.at[:, hc], spread.at[:, hc], net.at(h=1 - h))
-    t = net.send(spread.at[:, hc], spread.at[:, hc], net.at(c=1 - c))
-    yield
-    net.arrive(spread.at[:, (1 - h) * 2 + c], s)
-    u = net.send(spread.at[:, (1 - h) * 2 + c], spread.at[:, (1 - h) * 2 + c], net.at(c=1 - c))
-    net.arrive(spread.at[:, h * 2 + 1 - c], t)
-    net.arrive(spread.at[:, (1 - h) * 2 + 1 - c], u)
-
-    def pick(i, carry):
-        picked[i] = spread[src_z[i], src_hc[i]]
-        return carry
-
-    lax.fori_loop(0, NZ, pick, 0)
-    yield
-    sems, keeps = [], []
-    mine = pl.ds(pl.multiple_of(z * n, n), n)
-    for k in range(NZ):
-        zt = net.dz(k)
-        for m in range(2):
-            if k == 0:
-                copy = pltpu.make_async_copy(picked.at[z, m], moved.at[m, mine], local_sems.at[m])
-                copy.start()
-                keeps.append(copy)
-            else:
-                sems.append((-k, m, net.send(picked.at[zt, m], moved.at[m, mine], net.at(z=zt))))
-    for copy in keeps:
-        copy.wait()
-    yield
-    for k, m, sem in sems:
-        net.arrive(moved.at[m, pl.ds(pl.multiple_of(net.dz(k) * n, n), n)], sem)
-    yield
+    )(*args)
 
 
 def add_into(dst, *srcs):
@@ -537,14 +554,19 @@
     b_first, b_last = pl.ds(HALF, QUART), pl.ds(HALF + QUART, QUART)
     both = slice(None)
     core, yb = {}, {}
-    for k in (4, 3, -3, 2, -2, 1, -1, 0):
-        zt = net.dz(k)
-        to_core[zt] = contribution((1 - c) * NZ + zt).astype(BF).reshape(2, TOK, width)
-        core[k] = net.send(to_core.at[zt], from_core.at[zt], other_c)
+
+    def give(s):
+        for k in ((4,), (3, -3), (2, -2), (1, -1), (0,), ())[s]:
+            zt = net.dz(k)
+            to_core[zt] = contribution((1 - c) * NZ + zt).astype(BF).reshape(2, TOK, width)
+            core[k] = net.send(to_core.at[zt], from_core.at[zt], other_c)
+
+    give(0)
     yield
     ar = al = br = bl = None
     for s in range(5):
         ks = (4,) if s == 0 else (0,) if s == 4 else (4 - s, s - 4)
+        give(s + 1)
         for k in ks:
             zt = net.dz(k)
             net.arrive(from_core.at[zt], core[k])
@@ -600,28 +622,37 @@
     yield
 
 
+ORDER = "bmf" "bf" "bf" "mhbf" "hbf" "mhbf" "mhsbf" "hsbd" "sb" "sb" "sb" "bg"
+
+
 def finish_kernel(
-    hid_s, slope_s, rows_new, cot_new, rank, weight, wg, wd, src_z, src_hc,
+    slope_s, hidden, hid_moved, rows_new, cot_new, rank, weight, wg, wd, old, new,
     layer_out, token_grads, grad_gate, grad_down,
-    hidden, slope, hidden_new, slope_new, spread, picked, moved, out_rows, back_rows,
+    slope, hidden_new, slope_new, spread, picked, moved, out_rows, back_rows,
     to_core, from_core, sums, y_b, ring_ra, ring_la, ring_rb, ring_lb, y_a,
     local_sem, send_sem, recv_sem,
 ):
     net = Links(send_sem, recv_sem)
-    net.barrier(all_z=True)
-    whole_h = whole_flow(net, hid_s, hidden, local_sem.at[0])
-    whole_s = whole_flow(net, slope_s, slope, local_sem.at[1])
-    move = move_flow(net, hid_s, slope_s, src_z, src_hc, spread, picked, moved, local_sem.at[pl.ds(2, 2)])
+    net.barrier()
+    tile = 320
 
     def weighted(i, carry):
-        at = pl.ds(pl.multiple_of(i * PAIR, 16), PAIR)
-        w = jnp.sum(picker(rank, i) * weight[pl.ds(i, 1), :], axis=1, keepdims=True)
+        at = pl.ds(pl.multiple_of(i * tile, tile), tile)
+        w = jnp.concatenate(
+            [
+                jnp.sum(
+                    picker(rank, i * 4 + j) * weight[pl.ds(i * 4 + j, 1), :], axis=1, keepdims=True
+                )
+                for j in range(4)
+            ],
+            axis=0,
+        )
         out = jnp.dot(hidden[at, :], wd[...], preferred_element_type=F32)
         out_rows[at, :] = (out * w).astype(BF)
         return carry
 
     def plain(i, carry):
-        at = pl.ds(pl.multiple_of(i * 160, 160), 160)
+        at = pl.ds(pl.multiple_of(i * tile, tile), tile)
         back_rows[at, :] = jnp.dot(slope[at, :], wg[...], preferred_element_type=F32).astype(BF)
         return carry
 
@@ -635,47 +666,44 @@
 
     def outer(left, right, out):
         def body(i, carry):
-            at = pl.ds(pl.multiple_of(i * 128, 128), 128)
+            at = pl.ds(pl.multiple_of(i * 256, 256), 256)
             out[at, :] = lax.dot_general(
                 left[:, at], right[...], (((0,), (0,)), ((), ())), preferred_element_type=F32
             ).astype(BF)
             return carry
 
-        lax.fori_loop(0, 8, body, 0)
+        lax.fori_loop(0, 4, body, 0)
 
     bufs = (to_core, from_core, sums, y_b, ring_ra, ring_la, ring_rb, ring_lb, y_a)
 
     def forward():
-        yield from whole_h
-        lax.fori_loop(0, 16, weighted, 0)
+        lax.fori_loop(0, ROWS // tile, weighted, 0)
         yield from return_flow(net, placed(out_rows), *[b.at[0] for b in bufs], layer_out)
 
     def backward():
-        yield from whole_s
-        lax.fori_loop(0, ROWS // 160, plain, 0)
+        yield from whole_flow(net, slope_s, slope, local_sem.at[0])
+        lax.fori_loop(0, ROWS // tile, plain, 0)
         yield from return_flow(net, placed(back_rows), *[b.at[1] for b in bufs], token_grads)
 
-    def grads():
-        yield from move
-        first = whole_flow(net, moved.at[1], slope_new, local_sem.at[0])
-        second = whole_flow(net, moved.at[0], hidden_new, local_sem.at[1])
-        next(first)
-        next(second)
-        for _ in range(5):
-            next(first)
-            next(second)
-            yield
-        outer(slope_new, rows_new, grad_gate)
-        yield
-        outer(hidden_new, cot_new, grad_down)
-        yield
-
-    run_together(forward(), backward(), grads())
+    flows = {
+        "b": backward(),
+        "f": forward(),
+        "m": move_flow(net, slope_s, old, new, spread, picked, moved, local_sem.at[1]),
+        "h": whole_flow(net, hid_moved, hidden_new, local_sem.at[2]),
+        "s": whole_flow(net, moved, slope_new, local_sem.at[3]),
+    }
+    for step in ORDER:
+        if step == "d":
+            outer(hidden_new, cot_new, grad_down)
+        elif step == "g":
+            outer(slope_new, rows_new, grad_gate)
+        else:
+            next(flows[step], None)
     net.drain()
 
 
 def finish(*args):
-    width = args[2].shape[1]
+    width = args[3].shape[1]
     vm = pl.BlockSpec(memory_space=pltpu.VMEM)
     sm = pl.BlockSpec(memory_space=pltpu.SMEM)
     sds = jax.ShapeDtypeStruct
@@ -688,16 +716,15 @@
             sds((1024, width), BF),
             sds((1024, width), BF),
         ),
-        in_specs=[vm] * 8 + [sm] * 2,
+        in_specs=[vm] * 9 + [sm] * 2,
         out_specs=(vm,) * 4,
         scratch_shapes=[
             pltpu.VMEM((ROWS, 1024), BF),
             pltpu.VMEM((ROWS, 1024), BF),
             pltpu.VMEM((ROWS, 1024), BF),
-            pltpu.VMEM((ROWS, 1024), BF),
-            pltpu.VMEM((NZ, 4, 2, n, 128), BF),
-            pltpu.VMEM((NZ, 2, n, 128), BF),
-            pltpu.VMEM((2, ROWS, 128), BF),
+            pltpu.VMEM((NZ, 4, n, 128), BF),
+            pltpu.VMEM((NZ, n, 128), BF),
+            pltpu.VMEM((ROWS, 128), BF),
             pltpu.VMEM((ROWS, width), BF),
             pltpu.VMEM((ROWS, width), BF),
             pltpu.VMEM((2, NZ, 2, TOK, width), BF),
@@ -720,21 +747,13 @@
 
 
 def per_device(tokens, cotangent, expert_ids, gate_weights, owner_old, owner_new, w_gate, w_down):
-    me = lax.axis_index("expert")
-    labels = jnp.arange(32, dtype=jnp.int32)
     info = jnp.concatenate([expert_ids.T.astype(F32), gate_weights.T], axis=0)
-    eold = jnp.broadcast_to(jnp.sum(jnp.where(owner_old == me, labels, 0)).astype(F32), (8, 128))
-    enew = jnp.broadcast_to(jnp.sum(jnp.where(owner_new == me, labels, 0)).astype(F32), (8, 128))
-    lane = jnp.arange(128)
-    tri = (lane[:, None] < lane[None, :]).astype(BF)
-    targets = jnp.arange(NZ, dtype=jnp.int32) * 4 + me % 4
-    source = jnp.sum(jnp.where(owner_new[None, :] == targets[:, None], owner_old[None, :], 0), axis=1)
     gate_here, down_here = w_gate[0], w_down[0]
-    hid_s, slope_s, rows_new, cot_new, rank, weight = dispatch(
-        tokens, cotangent, info, gate_here, down_here, eold, enew, tri
+    slope_s, hidden, hid_moved, rows_new, cot_new, rank, weight = dispatch(
+        tokens, cotangent, info, gate_here, down_here, owner_old, owner_new
     )
     layer_out, token_grads, grad_gate, grad_down = finish(
-        hid_s, slope_s, rows_new, cot_new, rank, weight, gate_here, down_here, source // 4, source % 4
+        slope_s, hidden, hid_moved, rows_new, cot_new, rank, weight, gate_here, down_here, owner_old, owner_new
     )
     return (layer_out, token_grads, grad_gate[None], grad_down[None])
 

time: 343 us -> 289 us (0.84)
  Pallas kernels: 325 us -> 278 us
    pallas_call x1, Pallas kernels: 185 us -> 129 us  [finish(): pl.pallas_call(finish_kernel, out_shape=(sds((TOK, width), BF), sds((TOK,...]
    pallas_call x1, Pallas kernels: 140 us -> 149 us  [dispatch(): pl.pallas_call(dispatch_kernel, out_shape=(sds((ROWS, 128), BF), sds((ROW...]
where the time goes in v3:
time: 289 us; the launch traced here: 288 us
  Pallas kernels  278 us (96%)
  local copies, waits for them, and re-layouts  7.53 us (3%)
    pallas_call x1, Pallas kernels, dispatch(): pl.pallas_call(dispatch_kernel, out_shape=(sds((ROWS, 128), BF), sds((ROW...  149 us
    pallas_call x1, Pallas kernels, finish(): pl.pallas_call(finish_kernel, out_shape=(sds((TOK, width), BF), sds((TOK,...  129 us
    unnamed x6, local copies, waits for them, and re-layouts  7.53 us

profile of v3, /device:TPU:8, one launch (start us, length us, event | category | flops | bytes accessed | tf_op | source)
XLA Modules:
  0.0 288.3 jit_solution(14799269102031089753)
XLA Ops:
  0.6 0.7 convert_bitcast_fusion
  1.3 1.3 pad_maximum_fusion.info
  2.6 148.9 %shard_map.111 = (bf16[1280,128]{1,0:T(8,128)(2,1)}, bf16[1280,1024]{1,0:T(8,128)(2,1)}, bf16[1280,128]{1,0:T(8,128)(2,1)}, bf16[1280,896]{1,0:T(8,128)(2,1)}, b...) custom-call(bf16[128,896]{1,0:T(8,128)(2,1)} %tok.1, bf16[128,896]{1,0:T(8,128)(2,1)} %cot.1, ...), custom_call_target="tpu_custom_call" | custom-call | tf_op jit(solution)/shard_map/pallas_call | solution.py:488
  151.5 129.3 %shard_map.112 = (bf16[128,896]{1,0:T(8,128)(2,1)}, bf16[128,896]{1,0:T(8,128)(2,1)}, bf16[1024,896]{1,0:T(8,128)(2,1)}, bf16[1024,896]{1,0:T(8,128)(2,1)}) custom-call(bf16[1280,128]{1,0:T(8,128)(2,1)} %get-tuple-element.15.slope_s, bf16[1280,1024]{1,0:T(8,128)(2,1)} %get-tuple-element.16.hidden, bf16[1280,128]{1,0:T(8,128)(2,1)} %get-tuple-element.17.hid_moved, ...), custom_call_target="tpu_custom_call" | custom-call | tf_op jit(solution)/shard_map/pallas_call | solution.py:711
  280.8 1.6 copy.16
  282.4 1.6 copy.17
  284.0 0.0 copy-start
  284.0 3.0 %copy.18 = bf16[1,1024,896]{2,1,0:T(8,128)(2,1)} copy(bf16[1,1024,896]{2,1,0:T(8,128)(2,1)} %bitcast.12) | data formatting | bytes 3670016
  287.1 0.0 copy-done
  287.1 1.2 copy.19
Async XLA Ops:
  284.0 3.0 %copy-start = (bf16[1024,896]{1,0:T(8,128)(2,1)S(1)}, bf16[1024,896]{1,0:T(8,128)(2,1)}, u32[]{:S(2)}) copy-start(bf16[1024,896]{1,0:T(8,128)(2,1)} %get-tuple-element.25) | copy-start | bytes 5505028

commit v4 on v3

--- a/solution.py
+++ b/solution.py
@@ -12,7 +12,8 @@
 F32 = jnp.float32
 VMEM_LIMIT = 62 << 20
 NZ, CAP, TOK, HALF, QUART = 8, 40, 128, 64, 32
-ROWS, PAIR = 1280, 80
+ROWS, PAIR, CHUNK = 1280, 80, 640
+NEAR = (0, -1, 1, -2, 2, -3, 3, 4)
 
 
 def place():
@@ -80,7 +81,7 @@
         self.sent = []
 
 
-def gather_flow(net, own, full, local_sem):
+def gather_flow(net, own, full, local_sem, core_sems):
     z, h, c = net.z, net.h, net.c
     other_y, other_c = net.at(h=1 - h), net.at(c=1 - c)
     right, left = net.at(z=net.dz(1)), net.at(z=net.dz(-1))
@@ -88,7 +89,6 @@
     ra, rb = pl.ds(0, HALF), pl.ds(HALF, HALF)
     a_first, a_last = pl.ds(0, QUART), pl.ds(QUART, QUART)
     b_first, b_last = pl.ds(HALF, QUART), pl.ds(HALF + QUART, QUART)
-    core_sems = [net.new() for _ in range(NZ)]
     keep = pltpu.make_async_copy(own, full.at[me, h], local_sem)
     keep.start()
     ya = net.send(own.at[ra], full.at[me, h, ra], other_y)
@@ -148,8 +148,6 @@
         slot = c * NZ + net.dz(d)
         net.arrive(full.at[slot, 1 - h, rb], sem)
         to_core(d, (1 - h, rb))
-    for k in range(NZ):
-        net.arrive(full.at[(1 - c) * NZ + net.dz(k)], core_sems[k])
     yield
 
 
@@ -186,11 +184,12 @@
     return pl.ds(pl.multiple_of(xt * 256 + lo * 128, 128), 128)
 
 
-def reduce_flow(net, part, out, hop_r, hop_l, in_r, in_l, y_out, y_in):
+def reduce_flow(net, part, out, hop_r, hop_l, in_r, in_l, y_out, y_in, start):
     x, lo = net.x, net.lo
     right, left = net.at(x=net.dx(1)), net.at(x=net.dx(-1))
-    n = ROWS // 2
-    r0, r1 = pl.ds(0, n), pl.ds(n, n)
+    n = CHUNK // 2
+    r0, r1 = pl.ds(start, n), pl.ds(start + n, n)
+    hop_r, hop_l = hop_r.at[pl.ds(start // 2, n)], hop_l.at[pl.ds(start // 2, n)]
     far, nr, nl, own = cols(net.dx(2)), cols(net.dx(1)), cols(net.dx(-1)), cols(x)
     s1 = net.send(part.at[r0, far], hop_r, right)
     s2 = net.send(part.at[r1, far], hop_l, left)
@@ -212,10 +211,10 @@
         lax.fori_loop(0, n // tile, body, 0)
 
     net.arrive(hop_r, s1)
-    add(0, nr, hop_r)
+    add(start, nr, hop_r)
     s5 = net.send(part.at[r0, nr], in_r.at[r0], right)
     net.arrive(hop_l, s2)
-    add(n, nl, hop_l)
+    add(start + n, nl, hop_l)
     s6 = net.send(part.at[r1, nl], in_l.at[r1], left)
     yield
     waits = {0: ((in_r, s5), (in_l, s4)), 1: ((in_r, s3), (in_l, s6))}
@@ -226,7 +225,7 @@
             net.arrive(buf.at[rows_half], sem)
 
         def total(i, carry):
-            rows = pl.ds(pl.multiple_of(half * n + i * tile, tile), tile)
+            rows = pl.ds(pl.multiple_of(start + half * n + i * tile, tile), tile)
             for side, keep in ((lo, True), (1 - lo, False)):
                 inner = pl.ds(pl.multiple_of(side * 128, 128), 128)
                 acc = (
@@ -242,12 +241,12 @@
 
         lax.fori_loop(0, n // tile, total, 0)
         ys.append((half, net.send(y_out.at[rows_half], y_in.at[rows_half], net.at(lo=1 - lo))))
-        yield
+    yield
     for half, sem in ys:
         net.arrive(y_in.at[(r0, r1)[half]], sem)
 
         def last(i, carry):
-            rows = pl.ds(pl.multiple_of(half * n + i * tile, tile), tile)
+            rows = pl.ds(pl.multiple_of(start + half * n + i * tile, tile), tile)
             out[rows, :] = out[rows, :] + y_in[rows, :].astype(F32)
             return carry
 
@@ -383,99 +382,134 @@
     return jnp.where(slots == rank_ref[pl.ds(p, 1), :], 1.0, 0.0)
 
 
+FIRST = "it" "it" "itk" "ikt" "ikir" "p" "tpkt" "qpu" "pq" "k" "qqhwm" "ku" "w" "v" "um" "w" "v" "u" "mw" "v" "w" "vm"
+
+
 def dispatch_kernel(
-    tok, cot, info, wg, wd, old, new,
-    slope_o, hidden, hid_moved, rows_new, cot_new, rank_old, weight_old,
-    tok_all, cot_all, info_all, rows, part_a, part_b, acc_a, acc_b,
+    tok, cot, info, wg_in, wd_in, old, new,
+    slope_o, hidden_o, hid_moved, rows_new_o, cot_new_o, rank_old, weight_old,
+    wg, wd, hidden, rows_new, cot_new, tok_all, cot_all, info_all, rows, rows_b, part_a, part_b, acc_a, acc_b,
     hop_r, hop_l, in_r, in_l, y_out, y_in,
     rank_new, weight_new, hid_s, spread, picked,
     local_sem, send_sem, recv_sem,
 ):
     net = Links(send_sem, recv_sem)
+    load_g = pltpu.make_async_copy(wg_in, wg, local_sem.at[3])
+    load_d = pltpu.make_async_copy(wd_in, wd, local_sem.at[4])
+    keep_rows = pltpu.make_async_copy(rows_new, rows_new_o, local_sem.at[5])
+    keep_cot = pltpu.make_async_copy(cot_new, cot_new_o, local_sem.at[6])
+    keep_hidden = pltpu.make_async_copy(hidden, hidden_o, local_sem.at[7])
+    load_g.start()
+    load_d.start()
     net.barrier()
-    small = small_gather(net, info, info_all, local_sem.at[0])
-    toks = gather_flow(net, tok, tok_all, local_sem.at[1])
-    cots = later(2, gather_flow(net, cot, cot_all, local_sem.at[2]))
-    for turn, _ in enumerate(together(small, toks)):
-        if turn < 6:
-            next(cots)
-    me = net.z * 4 + net.h * 2 + net.c
-    ranks(info_all, look_up(old, me, jnp.int32), rank_old, weight_old)
-    ranks(info_all, look_up(new, me, jnp.int32), rank_new, weight_new)
-
-    def pick_tok(p, carry):
-        block = tok_all[p].reshape(2 * TOK, tok_all.shape[-1])
-        at = pl.ds(pl.multiple_of(p * PAIR, 16), PAIR)
-        for rank_ref, out in ((rank_old, rows), (rank_new, rows_new)):
-            sel = picker(rank_ref, p).astype(BF)
-            out[at, :] = jnp.dot(sel, block, preferred_element_type=F32).astype(BF)
-        return carry
-
-    def pick_cot(p, carry):
-        block = cot_all[p].reshape(2 * TOK, cot_all.shape[-1])
-        at = pl.ds(pl.multiple_of(p * PAIR, 16), PAIR)
-        for rank_ref, weight_ref, out in ((rank_old, weight_old, rows), (rank_new, weight_new, cot_new)):
-            hit = picker(rank_ref, p)
-            weight = jnp.sum(hit * weight_ref[pl.ds(p, 1), :], axis=1, keepdims=True)
-            sel = jnp.dot(hit.astype(BF), block, preferred_element_type=F32)
-            out[at, :] = (sel * weight).astype(BF)
-        return carry
-
-    def project(w, part, shift):
+    tok_sems = [net.new() for _ in range(NZ)]
+    cot_sems = [net.new() for _ in range(NZ)]
+    bufs_a = [r.at[0] for r in (hop_r, hop_l, in_r, in_l, y_out, y_in)]
+    bufs_b = [r.at[1] for r in (hop_r, hop_l, in_r, in_l, y_out, y_in)]
+
+    def slabs(chunk):
+        return NEAR[:4] if chunk == 0 else NEAR[4:]
+
+    def landed(full, sems, chunk):
+        for k in slabs(chunk):
+            net.arrive(full.at[(1 - net.c) * NZ + net.dz(k)], sems[k % NZ])
+
+    def pairs(chunk):
+        for i, k in enumerate(slabs(chunk)):
+            for side in range(2):
+                yield (chunk * 8 + i * 2 + side) * PAIR, side * NZ + net.dz(k)
+
+    def pick_tok(chunk):
+        for near, p in pairs(chunk):
+            block = tok_all[p].reshape(2 * TOK, tok_all.shape[-1])
+            at = pl.ds(pl.multiple_of(p * PAIR, 16), PAIR)
+            sel = picker(rank_old, p).astype(BF)
+            rows[pl.ds(near, PAIR), :] = jnp.dot(sel, block, preferred_element_type=F32).astype(BF)
+            sel = picker(rank_new, p).astype(BF)
+            rows_new[at, :] = jnp.dot(sel, block, preferred_element_type=F32).astype(BF)
+
+    def pick_cot(chunk):
+        for near, p in pairs(chunk):
+            block = cot_all[p].reshape(2 * TOK, cot_all.shape[-1])
+            at = pl.ds(pl.multiple_of(p * PAIR, 16), PAIR)
+            for rank_ref, weight_ref, out, where in (
+                (rank_old, weight_old, rows_b, pl.ds(near, PAIR)),
+                (rank_new, weight_new, cot_new, at),
+            ):
+                hit = picker(rank_ref, p)
+                weight = jnp.sum(hit * weight_ref[pl.ds(p, 1), :], axis=1, keepdims=True)
+                sel = jnp.dot(hit.astype(BF), block, preferred_element_type=F32)
+                out[where, :] = (sel * weight).astype(BF)
+
+    def project(source, w, part, shift, chunk):
         where = cols(net.dx(shift))
         tile = 320
 
         def body(i, carry):
-            at = pl.ds(pl.multiple_of(i * tile, tile), tile)
+            at = pl.ds(pl.multiple_of(chunk * CHUNK + i * tile, tile), tile)
             part[at, where] = lax.dot_general(
-                rows[at, :], w[where, :], (((1,), (1,)), ((), ())), preferred_element_type=F32
+                source[at, :], w[where, :], (((1,), (1,)), ((), ())), preferred_element_type=F32
             ).astype(BF)
             return carry
 
-        lax.fori_loop(0, ROWS // tile, body, 0)
-
-    def flow(w, part, out, bufs):
-        project(w, part, 2)
-        red = reduce_flow(net, part, out, *bufs)
+        lax.fori_loop(0, CHUNK // tile, body, 0)
+
+    def flow(full, sems, pick, source, w, part, out, bufs, load, keep, chunk):
+        landed(full, sems, chunk)
+        pick(chunk)
+        if chunk == 0:
+            load.wait()
+        else:
+            keep.start()
+        project(source, w, part, 2, chunk)
+        red = reduce_flow(net, part, out, *bufs, chunk * CHUNK)
         next(red)
-        project(w, part, 1)
-        project(w, part, -1)
+        project(source, w, part, 1, chunk)
+        project(source, w, part, -1, chunk)
         next(red)
-        project(w, part, 0)
+        project(source, w, part, 0, chunk)
         yield
         yield from red
 
-    bufs_a = [r.at[0] for r in (hop_r, hop_l, in_r, in_l, y_out, y_in)]
-    bufs_b = [r.at[1] for r in (hop_r, hop_l, in_r, in_l, y_out, y_in)]
-    def act_hidden(i, carry):
-        at = pl.ds(pl.multiple_of(i * 160, 160), 160)
+    def spread_rows(out, value):
+        for chunk in range(2):
+            for near, p in pairs(chunk):
+                out[pl.ds(pl.multiple_of(p * PAIR, 16), PAIR), :] = value(pl.ds(near, PAIR)).astype(BF)
+
+    def act_hidden(at):
         pre = acc_a[at, :]
-        hid_s[at, :] = (pre * jax.nn.sigmoid(pre)).astype(BF)
-        return carry
-
-    def act_slope(i, carry):
-        at = pl.ds(pl.multiple_of(i * 160, 160), 160)
+        return pre * jax.nn.sigmoid(pre)
+
+    def act_slope(at):
         pre, back = acc_a[at, :], acc_b[at, :]
         sig = jax.nn.sigmoid(pre)
-        slope_o[at, :] = (back * sig * (1.0 + pre * (1.0 - sig))).astype(BF)
-        return carry
-
-    def pre_path():
-        lax.fori_loop(0, 16, pick_tok, 0)
-        yield from flow(wg, part_a, acc_a, bufs_a)
-        lax.fori_loop(0, ROWS // 160, act_hidden, 0)
-        yield from together(
-            whole_flow(net, hid_s, hidden, local_sem.at[1]),
-            move_flow(net, hid_s, old, new, spread, picked, hid_moved, local_sem.at[2]),
-        )
-
-    def back_path():
-        yield from cots
-        lax.fori_loop(0, 16, pick_cot, 0)
-        yield from flow(wd, part_b, acc_b, bufs_b)
-
-    run_together(pre_path(), back_path())
-    lax.fori_loop(0, ROWS // 160, act_slope, 0)
+        return back * sig * (1.0 + pre * (1.0 - sig))
+
+    flows = {
+        "i": small_gather(net, info, info_all, local_sem.at[0]),
+        "t": gather_flow(net, tok, tok_all, local_sem.at[1], tok_sems),
+        "k": gather_flow(net, cot, cot_all, local_sem.at[2], cot_sems),
+        "w": whole_flow(net, hid_s, hidden, local_sem.at[1]),
+        "m": move_flow(net, hid_s, old, new, spread, picked, hid_moved, local_sem.at[2]),
+    }
+    for name, chunk in (("p", 0), ("q", 1)):
+        flows[name] = flow(tok_all, tok_sems, pick_tok, rows, wg, part_a, acc_a, bufs_a, load_g, keep_rows, chunk)
+    for name, chunk in (("u", 0), ("v", 1)):
+        flows[name] = flow(cot_all, cot_sems, pick_cot, rows_b, wd, part_b, acc_b, bufs_b, load_d, keep_cot, chunk)
+    me = net.z * 4 + net.h * 2 + net.c
+    for step in FIRST:
+        if step == "r":
+            ranks(info_all, look_up(old, me, jnp.int32), rank_old, weight_old)
+            ranks(info_all, look_up(new, me, jnp.int32), rank_new, weight_new)
+        elif step == "h":
+            spread_rows(hid_s, act_hidden)
+        else:
+            next(flows[step], None)
+    keep_hidden.start()
+    spread_rows(slope_o, act_slope)
+    keep_rows.wait()
+    keep_cot.wait()
+    keep_hidden.wait()
     net.drain()
 
 
@@ -483,6 +517,7 @@
     width = args[0].shape[1]
     vm = pl.BlockSpec(memory_space=pltpu.VMEM)
     sm = pl.BlockSpec(memory_space=pltpu.SMEM)
+    hbm = pl.BlockSpec(memory_space=pl.ANY)
     sds = jax.ShapeDtypeStruct
     half = ROWS // 2
     return pl.pallas_call(
@@ -496,12 +531,18 @@
             sds((16, 256), F32),
             sds((16, 256), F32),
         ),
-        in_specs=[vm] * 5 + [sm] * 2,
-        out_specs=(vm,) * 7,
+        in_specs=[vm] * 3 + [hbm] * 2 + [sm] * 2,
+        out_specs=(vm, hbm, vm, hbm, hbm, vm, vm),
         scratch_shapes=[
+            pltpu.VMEM((1024, width), BF),
+            pltpu.VMEM((1024, width), BF),
+            pltpu.VMEM((ROWS, 1024), BF),
+            pltpu.VMEM((ROWS, width), BF),
+            pltpu.VMEM((ROWS, width), BF),
             pltpu.VMEM((16, 2, TOK, width), BF),
             pltpu.VMEM((16, 2, TOK, width), BF),
             pltpu.VMEM((2, 16, 16, 128), F32),
+            pltpu.VMEM((ROWS, width), BF),
             pltpu.VMEM((ROWS, width), BF),
             pltpu.VMEM((ROWS, 1024), BF),
             pltpu.VMEM((ROWS, 1024), BF),
@@ -518,7 +559,7 @@
             pltpu.VMEM((ROWS, 128), BF),
             pltpu.VMEM((NZ, 4, ROWS // NZ, 128), BF),
             pltpu.VMEM((NZ, ROWS // NZ, 128), BF),
-            pltpu.SemaphoreType.DMA((3,)),
+            pltpu.SemaphoreType.DMA((8,)),
             pltpu.SemaphoreType.DMA((256,)),
             pltpu.SemaphoreType.DMA((256,)),
         ],
@@ -626,13 +667,20 @@
 
 
 def finish_kernel(
-    slope_s, hidden, hid_moved, rows_new, cot_new, rank, weight, wg, wd, old, new,
+    slope_s, hidden, hid_moved, rows_in, cot_in, rank, weight, wg_in, wd_in, old, new,
     layer_out, token_grads, grad_gate, grad_down,
+    rows_new, cot_new, wg, wd,
     slope, hidden_new, slope_new, spread, picked, moved, out_rows, back_rows,
     to_core, from_core, sums, y_b, ring_ra, ring_la, ring_rb, ring_lb, y_a,
     local_sem, send_sem, recv_sem,
 ):
     net = Links(send_sem, recv_sem)
+    loads = [
+        pltpu.make_async_copy(src, dst, local_sem.at[4 + i])
+        for i, (src, dst) in enumerate(((wd_in, wd), (wg_in, wg), (cot_in, cot_new), (rows_in, rows_new)))
+    ]
+    for load in loads:
+        load.start()
     net.barrier()
     tile = 320
 
@@ -677,11 +725,13 @@
     bufs = (to_core, from_core, sums, y_b, ring_ra, ring_la, ring_rb, ring_lb, y_a)
 
     def forward():
+        loads[0].wait()
         lax.fori_loop(0, ROWS // tile, weighted, 0)
         yield from return_flow(net, placed(out_rows), *[b.at[0] for b in bufs], layer_out)
 
     def backward():
         yield from whole_flow(net, slope_s, slope, local_sem.at[0])
+        loads[1].wait()
         lax.fori_loop(0, ROWS // tile, plain, 0)
         yield from return_flow(net, placed(back_rows), *[b.at[1] for b in bufs], token_grads)
 
@@ -694,8 +744,10 @@
     }
     for step in ORDER:
         if step == "d":
+            loads[2].wait()
             outer(hidden_new, cot_new, grad_down)
         elif step == "g":
+            loads[3].wait()
             outer(slope_new, rows_new, grad_gate)
         else:
             next(flows[step], None)
@@ -706,6 +758,7 @@
     width = args[3].shape[1]
     vm = pl.BlockSpec(memory_space=pltpu.VMEM)
     sm = pl.BlockSpec(memory_space=pltpu.SMEM)
+    hbm = pl.BlockSpec(memory_space=pl.ANY)
     sds = jax.ShapeDtypeStruct
     n = ROWS // NZ
     return pl.pallas_call(
@@ -716,9 +769,13 @@
             sds((1024, width), BF),
             sds((1024, width), BF),
         ),
-        in_specs=[vm] * 9 + [sm] * 2,
+        in_specs=[vm] * 3 + [hbm] * 2 + [vm] * 2 + [hbm] * 2 + [sm] * 2,
         out_specs=(vm,) * 4,
         scratch_shapes=[
+            pltpu.VMEM((ROWS, width), BF),
+            pltpu.VMEM((ROWS, width), BF),
+            pltpu.VMEM((1024, width), BF),
+            pltpu.VMEM((1024, width), BF),
             pltpu.VMEM((ROWS, 1024), BF),
             pltpu.VMEM((ROWS, 1024), BF),
             pltpu.VMEM((ROWS, 1024), BF),
@@ -736,7 +793,7 @@
             pltpu.VMEM((2, 4, HALF, width), BF),
             pltpu.VMEM((2, 4, HALF, width), BF),
             pltpu.VMEM((2, HALF, width), BF),
-            pltpu.SemaphoreType.DMA((4,)),
+            pltpu.SemaphoreType.DMA((8,)),
             pltpu.SemaphoreType.DMA((256,)),
             pltpu.SemaphoreType.DMA((256,)),
         ],

time: 289 us -> 277 us (0.958)
  Pallas kernels: 278 us -> 267 us
    pallas_call x1, Pallas kernels: 149 us -> 142 us  [dispatch(): pl.pallas_call(dispatch_kernel, out_shape=(sds((ROWS, 128), BF), sds((ROW...]
    pallas_call x1, Pallas kernels: 129 us -> 125 us  [finish(): pl.pallas_call(finish_kernel, out_shape=(sds((TOK, width), BF), sds((TOK,...]
where the time goes in v4:
time: 277 us
  Pallas kernels  267 us (96%)
  local copies, waits for them, and re-layouts  7.53 us (3%)
    pallas_call x1, Pallas kernels, dispatch(): pl.pallas_call(dispatch_kernel, out_shape=(sds((ROWS, 128), BF), sds((ROW...  142 us
    pallas_call x1, Pallas kernels, finish(): pl.pallas_call(finish_kernel, out_shape=(sds((TOK, width), BF), sds((TOK,...  125 us
    unnamed x6, local copies, waits for them, and re-layouts  7.53 us

profile of v4, /device:TPU:8, one launch (start us, length us, event | category | flops | bytes accessed | tf_op | source)
XLA Modules:
  0.0 277.0 jit_solution(1632457357683854379)
XLA Ops:
  0.6 0.7 convert_bitcast_fusion
  1.3 1.3 pad_maximum_fusion.info
  2.6 141.5 %shard_map.111 = (bf16[1280,128]{1,0:T(8,128)(2,1)}, bf16[1280,1024]{1,0:T(8,128)(2,1)}, bf16[1280,128]{1,0:T(8,128)(2,1)}, bf16[1280,896]{1,0:T(8,128)(2,1)}, b...) custom-call(bf16[128,896]{1,0:T(8,128)(2,1)} %tok.1, bf16[128,896]{1,0:T(8,128)(2,1)} %cot.1, ...), custom_call_target="tpu_custom_call" | custom-call | tf_op jit(solution)/shard_map/pallas_call | solution.py:523
  144.1 125.4 %shard_map.112 = (bf16[128,896]{1,0:T(8,128)(2,1)}, bf16[128,896]{1,0:T(8,128)(2,1)}, bf16[1024,896]{1,0:T(8,128)(2,1)}, bf16[1024,896]{1,0:T(8,128)(2,1)}) custom-call(bf16[1280,128]{1,0:T(8,128)(2,1)} %get-tuple-element.15.slope_s, bf16[1280,1024]{1,0:T(8,128)(2,1)} %get-tuple-element.16.hidden, bf16[1280,128]{1,0:T(8,128)(2,1)} %get-tuple-element.17.hid_moved, ...), custom_call_target="tpu_custom_call" | custom-call | tf_op jit(solution)/shard_map/pallas_call | solution.py:764
  269.5 1.6 copy.16
  271.1 1.6 copy.17
  272.8 0.0 copy-start
  272.8 3.0 %copy.18 = bf16[1,1024,896]{2,1,0:T(8,128)(2,1)} copy(bf16[1,1024,896]{2,1,0:T(8,128)(2,1)} %bitcast.12) | data formatting | bytes 3670016
  275.8 0.0 copy-done
  275.8 1.2 copy.19
Async XLA Ops:
  272.8 3.0 %copy-start = (bf16[1024,896]{1,0:T(8,128)(2,1)S(1)}, bf16[1024,896]{1,0:T(8,128)(2,1)}, u32[]{:S(2)}) copy-start(bf16[1024,896]{1,0:T(8,128)(2,1)} %get-tuple-element.25) | copy-start | bytes 5505028

commit v5 on v4

--- a/solution.py
+++ b/solution.py
@@ -803,15 +803,47 @@
     )(*args)
 
 
+def hand_out_kernel(a, b, c, d, a_o, b_o, c_o, d_o, a_v, b_v, c_v, d_v, load_sem, store_sem):
+    loads, stores = [], []
+    for src, mid, dst, parts in ((c, c_v, c_o, 4), (d, d_v, d_o, 4), (a, a_v, a_o, 1), (b, b_v, b_o, 1)):
+        n = src.shape[0] // parts
+        for i in range(parts):
+            rows = pl.ds(i * n, n)
+            k = len(loads)
+            loads.append(pltpu.make_async_copy(src.at[rows], mid.at[rows], load_sem.at[k]))
+            stores.append(pltpu.make_async_copy(mid.at[rows], dst.at[rows], store_sem.at[k]))
+    for load in loads:
+        load.start()
+    for load, store in zip(loads, stores):
+        load.wait()
+        store.start()
+    for store in stores:
+        store.wait()
+
+
+def hand_out(*results):
+    hbm = pl.BlockSpec(memory_space=pl.ANY)
+    return pl.pallas_call(
+        hand_out_kernel,
+        out_shape=tuple(jax.ShapeDtypeStruct(r.shape, r.dtype) for r in results),
+        in_specs=[hbm] * 4,
+        out_specs=(hbm,) * 4,
+        scratch_shapes=[pltpu.VMEM(r.shape, r.dtype) for r in results]
+        + [pltpu.SemaphoreType.DMA((10,)), pltpu.SemaphoreType.DMA((10,))],
+        compiler_params=pltpu.CompilerParams(vmem_limit_bytes=VMEM_LIMIT),
+    )(*results)
+
+
 def per_device(tokens, cotangent, expert_ids, gate_weights, owner_old, owner_new, w_gate, w_down):
     info = jnp.concatenate([expert_ids.T.astype(F32), gate_weights.T], axis=0)
     gate_here, down_here = w_gate[0], w_down[0]
     slope_s, hidden, hid_moved, rows_new, cot_new, rank, weight = dispatch(
         tokens, cotangent, info, gate_here, down_here, owner_old, owner_new
     )
-    layer_out, token_grads, grad_gate, grad_down = finish(
+    results = finish(
         slope_s, hidden, hid_moved, rows_new, cot_new, rank, weight, gate_here, down_here, owner_old, owner_new
     )
+    layer_out, token_grads, grad_gate, grad_down = hand_out(*results)
     return (layer_out, token_grads, grad_gate[None], grad_down[None])
 
 

time: 277 us -> 273 us (0.986)
  local copies, waits for them, and re-layouts: 7.53 us -> 0 us
  Pallas kernels: 267 us -> 270 us
    unnamed x6 -> x0, local copies, waits for them, and re-layouts: 7.53 us -> none
    pallas_call x0 -> x1, Pallas kernels: none -> 3.5 us  [hand_out(): pl.pallas_call(hand_out_kernel, out_shape=tuple((jax.ShapeDtypeStruct(r.s...]
where the time goes in v5:
time: 273 us
  Pallas kernels  270 us (99%)
    pallas_call x1, Pallas kernels, dispatch(): pl.pallas_call(dispatch_kernel, out_shape=(sds((ROWS, 128), BF), sds((ROW...  142 us
    pallas_call x1, Pallas kernels, finish(): pl.pallas_call(finish_kernel, out_shape=(sds((TOK, width), BF), sds((TOK,...  125 us

profile of v5, /device:TPU:8, one launch (start us, length us, event | category | flops | bytes accessed | tf_op | source)
XLA Modules:
  0.0 273.2 jit_solution(15230850172918039706)
XLA Ops:
  0.6 0.7 convert_bitcast_fusion
  1.3 1.3 pad_maximum_fusion.info
  2.6 141.5 %shard_map.111 = (bf16[1280,128]{1,0:T(8,128)(2,1)}, bf16[1280,1024]{1,0:T(8,128)(2,1)}, bf16[1280,128]{1,0:T(8,128)(2,1)}, bf16[1280,896]{1,0:T(8,128)(2,1)}, b...) custom-call(bf16[128,896]{1,0:T(8,128)(2,1)} %tok.1, bf16[128,896]{1,0:T(8,128)(2,1)} %cot.1, ...), custom_call_target="tpu_custom_call" | custom-call | tf_op jit(solution)/shard_map/pallas_call | solution.py:523
  144.1 125.4 %shard_map.112 = (bf16[128,896]{1,0:T(8,128)(2,1)}, bf16[128,896]{1,0:T(8,128)(2,1)}, bf16[1024,896]{1,0:T(8,128)(2,1)}, bf16[1024,896]{1,0:T(8,128)(2,1)}) custom-call(bf16[1280,128]{1,0:T(8,128)(2,1)} %get-tuple-element.19.slope_s, bf16[1280,1024]{1,0:T(8,128)(2,1)} %get-tuple-element.20.hidden, bf16[1280,128]{1,0:T(8,128)(2,1)} %get-tuple-element.21.hid_moved, ...), custom_call_target="tpu_custom_call" | custom-call | tf_op jit(solution)/shard_map/pallas_call | solution.py:764
  269.5 3.5 %shard_map.113 = (bf16[128,896]{1,0:T(8,128)(2,1)}, bf16[128,896]{1,0:T(8,128)(2,1)}, bf16[1024,896]{1,0:T(8,128)(2,1)}, bf16[1024,896]{1,0:T(8,128)(2,1)}) custom-call(bf16[128,896]{1,0:T(8,128)(2,1)} %get-tuple-element.26.a, bf16[128,896]{1,0:T(8,128)(2,1)} %get-tuple-element.27.b, bf16[1024,896]{1,0:T(8,128)(2,1)} %get-tuple-element.28.c, ...), custom_call_target="tpu_custom_call" | custom-call | tf_op jit(solution)/shard_map/pallas_call | solution.py:826
